TPU v7x, 512 devices: a whole 4x8x8 slice. The times are simulated.
512 devices in a mesh: solve: 64 (over x, z, core), cross: 8 (over y).
Axes of the slice: x: 4, y: 8, z: 8, core: 2. Of those that a mesh axis runs over, the one named last changes fastest.
Arguments:
- thermal_state_pair: float32 [2, 1024, 8192], P(None, 'solve', 'cross'), may hold values from -4 to 6
- longitudinal_interface_transfer: float32 [2, 1024, 8192], P(None, 'solve', 'cross'), may hold values from 524 to 7489
- transverse_diffusivity_cells: float32 [2, 1024, 8192], P(None, 'solve', 'cross'), may hold values from 0.02 to 0.24
- sheet_exchange_coefficient: float32 [1024, 8192], P('solve', 'cross'), may hold values from 0.05 to 10
Outputs:
- solution: float32 [2, 1024, 8192], P(None, 'solve', 'cross')
All inputs are finite; a program needn't handle non-finite values.
Results may differ from a plain program's by a relative error of at most 0.0003.
Values sent between devices are 32-bit elements; how exact they have to be, the bound alone decides.
A program may use at most 128 MiB of HBM per device.

v0:
```python
import functools

import jax
import jax.numpy as jnp
from jax import lax
from jax.experimental import pallas as pl
from jax.experimental.pallas import tpu as pltpu
from jax.sharding import PartitionSpec as P

MESH = pl.DeviceIdType.MESH
ROWS, SUBS, LANES = 16, 8, 128
GROUP, OWNERS = 16, 8
LOADS, USED, SLOT = 4, 14, 16
FLAT = 2 * ROWS * SUBS


def inverse(coupling, first, second):
    scale = 1.0 / (coupling * (first + second) + first * second)
    return (coupling + second) * scale, coupling * scale, (coupling + first) * scale


def merge(left, right):
    ea1, ea2, sa, n11, n12, n21, n22, ec1, ec2, sc = left
    fa1, fa2, fs, m11, m12, m21, m22, fc1, fc2, gs = right
    eb1, eb2, sb = ec1 + fa1, ec2 + fa2, sc + fs
    r1 = eb1 + ((n11 + n21) + (m11 + m12))
    r2 = eb2 + ((n12 + n22) + (m21 + m22))
    i11, i12, i22 = inverse(sb, r1, r2)
    g11, g12 = n11 * i11 + n12 * i12, n11 * i12 + n12 * i22
    g21, g22 = n21 * i11 + n22 * i12, n21 * i12 + n22 * i22
    h11, h12 = i11 * m11 + i12 * m21, i11 * m12 + i12 * m22
    h21, h22 = i12 * m11 + i22 * m21, i12 * m12 + i22 * m22
    joined = (
        ea1 + (g11 * eb1 + g12 * eb2),
        ea2 + (g21 * eb1 + g22 * eb2),
        sa + (g11 * n21 + g12 * n22),
        g11 * m11 + g12 * m21,
        g11 * m12 + g12 * m22,
        g21 * m11 + g22 * m21,
        g21 * m12 + g22 * m22,
        fc1 + (h11 * eb1 + h21 * eb2),
        fc2 + (h12 * eb1 + h22 * eb2),
        gs + (m11 * h12 + m21 * h22),
    )
    return joined, (i11, i12, i22, g11, g12, g21, g22, h11, h12, h21, h22)


def merge_leaf(sa, sb, n1, n2, m1, m2):
    r1, r2 = 1.0 + (n1 + m1), 1.0 + (n2 + m2)
    i11, i12, i22 = inverse(sb, r1, r2)
    g11, g12, g21, g22 = n1 * i11, n1 * i12, n2 * i12, n2 * i22
    h11, h12, h21, h22 = i11 * m1, i12 * m2, i12 * m1, i22 * m2
    joined = (
        1.0 + (g11 + g12),
        1.0 + (g21 + g22),
        sa + g12 * n2,
        g11 * m1,
        g12 * m2,
        g21 * m1,
        g22 * m2,
        h11 + h21,
        h12 + h22,
        m1 * h12,
    )
    return joined, (i11, i12, i22, g11, g12, g21, g22, h11, h12, h21, h22)


def merge_loads(back, left, right):
    i11, i12, i22, g11, g12, g21, g22, h11, h12, h21, h22 = back
    a1, a2, b1, b2 = left
    c1, c2, d1, d2 = right
    b1, b2 = b1 + c1, b2 + c2
    loads = (
        a1 + (g11 * b1 + g12 * b2),
        a2 + (g21 * b1 + g22 * b2),
        d1 + (h11 * b1 + h21 * b2),
        d2 + (h12 * b1 + h22 * b2),
    )
    return loads, (i11 * b1 + i12 * b2, i12 * b1 + i22 * b2)


def merge_leaf_loads(back, a, b):
    i11, i12, i22, g11, g12, g21, g22, h11, h12, h21, h22 = back
    a1, a2 = a
    b1, b2 = b
    loads = (
        a1 + (g11 * b1 + g12 * b2),
        a2 + (g21 * b1 + g22 * b2),
        h11 * b1 + h21 * b2,
        h12 * b1 + h22 * b2,
    )
    return loads, (i11 * b1 + i12 * b2, i12 * b1 + i22 * b2)


def middle(back, own, before, after):
    g11, g12, g21, g22, h11, h12, h21, h22 = back[3:]
    a1, a2 = before
    c1, c2 = after
    return (
        own[0] + ((g11 * a1 + g21 * a2) + (h11 * c1 + h12 * c2)),
        own[1] + ((g12 * a1 + g22 * a2) + (h21 * c1 + h22 * c2)),
    )


def kernel(
    groups,
    temp_hbm,
    face_hbm,
    diff_hbm,
    sheet_hbm,
    out_ref,
    temp,
    face,
    diff,
    sheet,
    source,
    edge_send,
    edge_recv,
    part_send,
    part_recv,
    late_send,
    line_send,
    line_recv,
    pick,
    node_send,
    node_recv,
    in_sem,
    edge_ssem,
    edge_rsem,
    part_ssem,
    part_rsem,
    line_ssem,
    line_rsem,
    node_ssem,
    node_rsem,
):
    solve = lax.axis_index("solve")
    cross = lax.axis_index("cross")
    n_cross = lax.axis_size("cross")
    place = lax.rem(solve, GROUP)
    group = lax.div(solve, GROUP)
    base = solve - place

    loads_in = [
        pltpu.make_async_copy(src, dst, in_sem.at[i])
        for i, (src, dst) in enumerate(
            ((temp_hbm, temp), (diff_hbm, diff), (face_hbm, face), (sheet_hbm, sheet))
        )
    ]
    for copy in loads_in:
        copy.start()

    owner = place < OWNERS
    owners = [lax.rem(place + step, OWNERS) for step in (4, 5, 3, 6, 2, 7, 1, 0)]
    order = [8, 9, 7, 10, 6, 11, 5, 12, 4, 13, 3, 14, 2, 15, 1]
    mates = [lax.rem(place + step, GROUP) for step in order]
    others = [lax.rem(group + step, groups) for step in range(1, groups)]
    right = lax.rem(cross + 1, n_cross)
    left = lax.rem(cross + n_cross - 1, n_cross)

    barrier = pltpu.get_barrier_semaphore()
    for side in (left, right):
        pl.semaphore_signal(barrier, 1, device_id={"cross": side}, device_id_type=MESH)

    @pl.when(owner)
    def _():
        for mate in mates:
            pl.semaphore_signal(
                barrier, 1, device_id={"solve": base + mate}, device_id_type=MESH
            )
        for other in others:
            pl.semaphore_signal(
                barrier, 1, device_id={"solve": other * GROUP + place}, device_id_type=MESH
            )

    lane = lax.broadcasted_iota(jnp.int32, (SUBS, LANES), 1)
    sub = lax.broadcasted_iota(jnp.int32, (SUBS, LANES), 0)

    def spin(value, shift):
        return pltpu.roll(value, shift % LANES, 1)

    def tile(ref, block, column):
        return ref[pl.ds((block * SUBS + column) * SUBS, SUBS), :]

    loads_in[0].wait()
    loads_in[1].wait()
    edges = []
    for column, shift in ((0, 0), (SUBS - 1, 1)):
        packed = jnp.zeros((SUBS, LANES), jnp.float32)
        for j in range(8):
            part = tile(temp if j < 4 else diff, j % 4, column)
            packed = jnp.where(lane == j, spin(part, j + shift), packed)
        edges.append(packed)
    edge_send[0] = edges[0]
    edge_send[1] = edges[1]

    zero = jnp.zeros((SUBS, LANES), jnp.float32)
    for block in range(4):
        heat = [tile(temp, block, t) for t in range(SUBS)]
        cond = [tile(diff, block, t) for t in range(SUBS)]
        heat_turned = [spin(v, -1) for v in heat] + [zero]
        cond_turned = [spin(v, -1) for v in cond] + [zero]
        last = lane == LANES - 1
        before = zero
        for t in range(SUBS):
            next_heat = jnp.where(last, heat_turned[t + 1], heat_turned[t])
            next_cond = jnp.where(last, cond_turned[t + 1], cond_turned[t])
            flux = 0.5 * (cond[t] + next_cond) * (next_heat - heat[t])
            if t == SUBS - 1:
                flux = jnp.where(last, 0.0, flux)
            turned = spin(flux, 1)
            previous = jnp.where(lane == 0, before, turned)
            before = turned
            source[pl.ds((block * SUBS + t) * SUBS, SUBS), :] = heat[t] + flux - previous

    def row(ref, plane, i):
        start = (plane * 2 + i // SUBS) * SUBS * SUBS + i % SUBS
        return ref[pl.ds(start, SUBS, stride=SUBS), :]

    loads_in[2].wait()
    loads_in[3].wait()
    backs = []
    level = []
    back = []
    for m in range(ROWS // 2):
        element, way = merge_leaf(
            row(sheet, 0, 2 * m),
            row(sheet, 0, 2 * m + 1),
            row(face, 0, 2 * m),
            row(face, 1, 2 * m),
            row(face, 0, 2 * m + 1),
            row(face, 1, 2 * m + 1),
        )
        level.append(element)
        back.append(way)
    backs.append(back)
    while len(level) > 1:
        pairs = [merge(level[2 * m], level[2 * m + 1]) for m in range(len(level) // 2)]
        level = [pair[0] for pair in pairs]
        backs.append([pair[1] for pair in pairs])
    element = level[0]

    def climb_loads():
        owns = []
        level = []
        own = []
        for m in range(ROWS // 2):
            loads, value = merge_leaf_loads(
                backs[0][m],
                (row(source, 0, 2 * m), row(source, 1, 2 * m)),
                (row(source, 0, 2 * m + 1), row(source, 1, 2 * m + 1)),
            )
            level.append(loads)
            own.append(value)
        owns.append(own)
        for back in backs[1:]:
            pairs = [
                merge_loads(back[m], level[2 * m], level[2 * m + 1]) for m in range(len(back))
            ]
            level = [pair[0] for pair in pairs]
            owns.append([pair[1] for pair in pairs])
        return level[0], owns

    def slot(ref, index, rows, used, skip=0):
        return ref.at[pl.ds(pl.multiple_of(index * rows, rows) + skip, used)]

    loads, _ = climb_loads()
    for j, value in enumerate(loads + element):
        part_send[pl.ds(j, SUBS, stride=SLOT), :] = value

    @pl.when(owner)
    def _():
        pl.semaphore_wait(barrier, 2 + OWNERS - 1 + len(others))

    @pl.when(jnp.logical_not(owner))
    def _():
        pl.semaphore_wait(barrier, 2 + OWNERS)

    edge_copies = [
        pltpu.make_async_remote_copy(
            src_ref=edge_send.at[i],
            dst_ref=edge_recv.at[i],
            send_sem=edge_ssem.at[i],
            recv_sem=edge_rsem.at[i],
            device_id={"cross": side},
            device_id_type=MESH,
        )
        for i, side in enumerate((left, right))
    ]
    for copy in edge_copies:
        copy.start()

    def part_copy(mate, skip, used):
        return pltpu.make_async_remote_copy(
            src_ref=slot(part_send, mate, SLOT, used, skip),
            dst_ref=slot(part_recv, place, SLOT, used, skip),
            send_sem=part_ssem,
            recv_sem=part_rsem,
            device_id={"solve": base + mate},
            device_id_type=MESH,
        )

    for mate in owners:
        outer = (mate == 0) | (mate == OWNERS - 1)

        @pl.when(outer & (mate != place))
        def _():
            part_copy(mate, LOADS, USED - LOADS).start()

        @pl.when(jnp.logical_not(outer) & (mate != place))
        def _():
            part_copy(mate, 0, USED).start()

    @pl.when(owner)
    def _():
        here = pl.ds(pl.multiple_of(place * SLOT, SLOT), USED)
        part_recv[here, :] = part_send[here, :]

    for i in (0, 1):
        edge_copies[i].wait_recv()
    for column, own, got, inside in (
        (0, edges[0], edge_recv[1], cross > 0),
        (SUBS - 1, edges[1], edge_recv[0], cross < n_cross - 1),
    ):
        got = jnp.where(inside, got, 0.0)
        flux = 0.5 * spin(own + got, -4) * (got - own)
        at = 0 if column == 0 else LANES - 1
        for j in range(4):
            where = pl.ds((j * SUBS + column) * SUBS, SUBS)
            source[where, :] += jnp.where(lane == at, spin(flux, at - j), 0.0)

    loads, owns = climb_loads()
    for j in range(LOADS):
        late_send[pl.ds(j, 1), :] = loads[j][0:1, :]
        late_send[pl.ds(LOADS + j, 1), :] = loads[j][SUBS - 1 : SUBS, :]
    for i, mate in enumerate((0, OWNERS - 1)):
        ready = pl.ds(i * LOADS, LOADS)

        @pl.when(place != mate)
        def _():
            pltpu.make_async_remote_copy(
                src_ref=late_send.at[ready],
                dst_ref=slot(part_recv, place, SLOT, LOADS),
                send_sem=part_ssem,
                recv_sem=part_rsem,
                device_id={"solve": base + mate},
                device_id_type=MESH,
            ).start()

        @pl.when(place == mate)
        def _():
            part_recv[pl.ds(mate * SLOT, LOADS), :] = late_send[ready, :]

    def climb(left_fields, right_fields):
        element, way = merge(left_fields[LOADS:], right_fields[LOADS:])
        loads, value = merge_loads(way, left_fields[:LOADS], right_fields[:LOADS])
        return loads + element, way, value

    @pl.when(owner)
    def _():
        everything = part_recv.at[pl.ds(0, (GROUP - 1) * USED)]
        pltpu.make_async_copy(everything, everything, part_rsem).wait()

        evens, odds = (
            tuple(part_recv[pl.ds(at + j, SUBS, stride=2 * SLOT), :] for j in range(USED))
            for at in (0, SLOT)
        )
        fields, way, value = climb(evens, odds)
        trail = [(way, value, 0)]
        for shift in (1, 2, 4):
            raised = tuple(pltpu.roll(v, SUBS - shift, 0) for v in fields)
            fields, way, value = climb(fields, raised)
            trail.append((way, value, shift))

        for j in range(USED):
            line_send[pl.ds(j, 1), :] = fields[j][0:1, :]
        line_copies = [
            pltpu.make_async_remote_copy(
                src_ref=line_send.at[pl.ds(0, USED)],
                dst_ref=slot(line_recv, group, SLOT, USED),
                send_sem=line_ssem,
                recv_sem=line_rsem,
                device_id={"solve": other * GROUP + place},
                device_id_type=MESH,
            )
            for other in others
        ]
        for copy in line_copies:
            copy.start()
        here = pl.ds(pl.multiple_of(group * SLOT, SLOT), USED)
        line_recv[here, :] = line_send[pl.ds(0, USED), :]
        everything = line_recv.at[pl.ds(0, (groups - 1) * USED)]
        pltpu.make_async_copy(everything, everything, line_rsem).wait()

        chain = []
        for g in range(groups):
            chain.append(tuple(line_recv[pl.ds(g * SLOT + j, 1), :] for j in range(USED)))
        steps = []
        while len(chain) > 1:
            joined = [climb(chain[2 * m], chain[2 * m + 1]) for m in range(len(chain) // 2)]
            steps.append([item[1:] for item in joined])
            chain = [item[0] for item in joined]
        f1, f2, _, _, ea1, ea2, sa, n11, n12, n21, n22, _, _, _ = chain[0]
        i11, i12, i22 = inverse(sa, ea1 + (n11 + n12), ea2 + (n21 + n22))
        nothing = jnp.zeros_like(f1)
        nodes = [(i11 * f1 + i12 * f2, i12 * f1 + i22 * f2), (nothing, nothing)]
        for step in reversed(steps):
            finer = []
            for m, (way, value) in enumerate(step):
                finer += [nodes[m], middle(way, value, nodes[m], nodes[m + 1])]
            nodes = finer + [nodes[-1]]
        for plane in (0, 1):
            for g in range(groups + 1):
                pick[plane, pl.ds(g, 1), :] = nodes[g][plane]
        before, after = (
            tuple(
                jnp.broadcast_to(pick[plane, pl.ds(group + step, 1), :], (SUBS, LANES))
                for plane in (0, 1)
            )
            for step in (0, 1)
        )

        for way, value, shift in reversed(trail):
            inner = middle(way, value, before, after)
            if shift == 0:
                break
            first = (sub & shift) == 0
            before = tuple(
                jnp.where(first, b, pltpu.roll(v, shift, 0)) for b, v in zip(before, inner)
            )
            after = tuple(
                jnp.where(first, v, pltpu.roll(a, shift, 0)) for v, a in zip(inner, after)
            )
        for j, value in enumerate(before + inner + inner + after):
            node_send[pl.ds(j, SUBS, stride=2 * LOADS), :] = value
        node_copies = [
            pltpu.make_async_remote_copy(
                src_ref=slot(node_send, mate, LOADS, LOADS),
                dst_ref=slot(node_recv, place, LOADS, LOADS),
                send_sem=node_ssem,
                recv_sem=node_rsem,
                device_id={"solve": base + mate},
                device_id_type=MESH,
            )
            for mate in mates
        ]
        for copy in node_copies:
            copy.start()
        here = pl.ds(pl.multiple_of(place * LOADS, LOADS), LOADS)
        node_recv[here, :] = node_send[here, :]

    def wait_for(ref, rows, sem):
        part = ref.at[pl.ds(0, rows)]
        pltpu.make_async_copy(part, part, sem).wait()

    @pl.when(owner)
    def _():
        wait_for(node_recv, (OWNERS - 1) * LOADS, node_rsem)

    @pl.when(jnp.logical_not(owner))
    def _():
        wait_for(node_recv, OWNERS * LOADS, node_rsem)

    values = [node_recv[pl.ds(j, SUBS, stride=LOADS), :] for j in range(LOADS)]
    ends = [tuple(values[:2]), tuple(values[2:])]

    nodes = ends
    for back, own in zip(reversed(backs), reversed(owns)):
        finer = []
        for m in range(len(back)):
            finer += [nodes[m], middle(back[m], own[m], nodes[m], nodes[m + 1])]
        nodes = finer + [nodes[-1]]
    for i in range(ROWS):
        for plane in (0, 1):
            start = (plane * 2 + i // SUBS) * SUBS * SUBS + i % SUBS
            out_ref[pl.ds(start, SUBS, stride=SUBS), :] = nodes[i][plane]

    for copy in edge_copies:
        copy.wait_send()
    @pl.when(owner)
    def _():
        wait_for(part_send, (OWNERS - 1) * USED, part_ssem)
        wait_for(line_recv, (groups - 1) * USED, line_ssem)
        wait_for(node_send, (GROUP - 1) * LOADS, node_ssem)

    @pl.when(jnp.logical_not(owner))
    def _():
        wait_for(part_send, OWNERS * USED, part_ssem)


def tiles(array):
    array = array.reshape(-1, ROWS // SUBS, SUBS, SUBS, LANES)
    return array.transpose(0, 1, 3, 2, 4).reshape(-1, LANES)


def per_device(temperature, transfer, diffusivity, exchange):
    groups = lax.axis_size("solve") // GROUP
    vmem = lambda *shape: pltpu.VMEM(shape, jnp.float32)
    dma = pltpu.SemaphoreType.DMA
    out = pl.pallas_call(
        functools.partial(kernel, groups),
        out_shape=jax.ShapeDtypeStruct((FLAT, LANES), jnp.float32),
        in_specs=[pl.BlockSpec(memory_space=pltpu.HBM)] * 4,
        out_specs=pl.BlockSpec(memory_space=pltpu.VMEM),
        scratch_shapes=[
            vmem(FLAT, LANES),
            vmem(FLAT, LANES),
            vmem(FLAT, LANES),
            vmem(FLAT // 2, LANES),
            vmem(FLAT, LANES),
            vmem(2, SUBS, LANES),
            vmem(2, SUBS, LANES),
            vmem(OWNERS * SLOT, LANES),
            vmem(GROUP * SLOT, LANES),
            vmem(2 * LOADS, LANES),
            vmem(SLOT, LANES),
            vmem(groups * SLOT, LANES),
            vmem(2, SUBS, LANES),
            vmem(GROUP * LOADS, LANES),
            vmem(OWNERS * LOADS, LANES),
            dma((4,)),
            dma((2,)),
            dma((2,)),
            dma,
            dma,
            dma,
            dma,
            dma,
            dma,
        ],
        compiler_params=pltpu.CompilerParams(
            collective_id=0, has_side_effects=True, vmem_limit_bytes=16 * 1024 * 1024
        ),
        cost_estimate=pl.CostEstimate(
            flops=4_000_000, bytes_accessed=600_000, transcendentals=0
        ),
        name="line_step",
    )(
        *(
            pltpu.with_memory_space_constraint(tiles(array), pltpu.HBM)
            for array in (temperature, transfer, diffusivity, exchange)
        )
    )
    out = out.reshape(2, ROWS // SUBS, SUBS, SUBS, LANES).transpose(0, 1, 3, 2, 4)
    return out.reshape(2, ROWS, SUBS * LANES)


def solution(mesh):
    specs = (P(None, "solve", "cross"),) * 3 + (P("solve", "cross"),)
    return jax.shard_map(
        per_device,
        mesh=mesh,
        in_specs=specs,
        out_specs=P(None, "solve", "cross"),
        check_vma=False,
    )
```

profile of v0, /device:TPU:1, one launch (start us, length us, event | category | flops | bytes accessed | tf_op | source)
XLA Modules:
  0.0 28.0 jit_solution(12461971212157900198)
XLA Ops:
  0.0 27.3 %line_step.1 = f32[256,128]{1,0:T(8,128)S(1)} custom-call(f32[256,128]{1,0:T(8,128)} %bitcast.26, f32[256,128]{1,0:T(8,128)} %bitcast.27, f32[256,128]{1,0:T(8,128)} %bitcast.28, f32[128,128]{1,0:T(8,128)} %bitcast.29), custom_call_target="tpu_custom_call" | custom-call | flops 4000000 | bytes 600000 | tf_op jit(solution)/shard_map/line_step/pallas_call | solution.py:500
  27.3 0.7 %copy.6 = f32[2,16,1024]{2,1,0:T(8,128)} copy(f32[2,16,1024]{2,1,0:T(8,128)S(1)} %bitcast.25) | data formatting | bytes 262144
where the time goes:
time: 28.1 us; the launch traced here: 28 us
  Pallas kernels  27.3 us (97%)
  local copies, waits for them, and re-layouts  0.66 us (2%)
    pallas_call x1, Pallas kernels, per_device(): pl.pallas_call(functools.partial(kernel, groups), out_shape=jax.ShapeDtyp...  27.3 us
    unnamed x1, local copies, waits for them, and re-layouts  0.66 us

commit v1 on v0

--- a/solution.py
+++ b/solution.py
@@ -115,10 +115,13 @@
     sheet,
     source,
     edge_send,
-    edge_recv,
+    edge_own,
+    edge_far,
+    flux_send,
+    flux_recv,
+    flipped,
     part_send,
     part_recv,
-    late_send,
     line_send,
     line_recv,
     pick,
@@ -126,7 +129,10 @@
     node_recv,
     in_sem,
     edge_ssem,
-    edge_rsem,
+    own_rsem,
+    far_rsem,
+    flux_ssem,
+    flux_rsem,
     part_ssem,
     part_rsem,
     line_ssem,
@@ -151,6 +157,7 @@
         copy.start()
 
     owner = place < OWNERS
+    outer = (place == 0) | (place == OWNERS - 1)
     owners = [lax.rem(place + step, OWNERS) for step in (4, 5, 3, 6, 2, 7, 1, 0)]
     order = [8, 9, 7, 10, 6, 11, 5, 12, 4, 13, 3, 14, 2, 15, 1]
     mates = [lax.rem(place + step, GROUP) for step in order]
@@ -159,8 +166,17 @@
     left = lax.rem(cross + n_cross - 1, n_cross)
 
     barrier = pltpu.get_barrier_semaphore()
-    for side in (left, right):
-        pl.semaphore_signal(barrier, 1, device_id={"cross": side}, device_id_type=MESH)
+    for column, side in ((0, left), (OWNERS - 1, right)):
+
+        @pl.when(place == column)
+        def _():
+            for mate in range(GROUP):
+                pl.semaphore_signal(
+                    barrier,
+                    1,
+                    device_id={"solve": base + mate, "cross": side},
+                    device_id_type=MESH,
+                )
 
     @pl.when(owner)
     def _():
@@ -182,17 +198,54 @@
     def tile(ref, block, column):
         return ref[pl.ds((block * SUBS + column) * SUBS, SUBS), :]
 
-    loads_in[0].wait()
-    loads_in[1].wait()
-    edges = []
-    for column, shift in ((0, 0), (SUBS - 1, 1)):
+    def slot(ref, index, rows, used, skip=0):
+        return ref.at[pl.ds(pl.multiple_of(index * rows, rows) + skip, used)]
+
+    for copy in loads_in:
+        copy.wait()
+    tracks = [(ref, j) for ref in (temp, diff, face) for j in range(4)]
+    tracks += [(sheet, 0), (sheet, 1)]
+    for i, (column, shift) in enumerate(((0, 0), (SUBS - 1, 1))):
         packed = jnp.zeros((SUBS, LANES), jnp.float32)
-        for j in range(8):
-            part = tile(temp if j < 4 else diff, j % 4, column)
-            packed = jnp.where(lane == j, spin(part, j + shift), packed)
-        edges.append(packed)
-    edge_send[0] = edges[0]
-    edge_send[1] = edges[1]
+        for j, (ref, block) in enumerate(tracks):
+            packed = jnp.where(lane == j, spin(tile(ref, block, column), j + shift), packed)
+        edge_send[pl.ds(i * SUBS, SUBS), :] = packed
+
+    @pl.when(owner)
+    def _():
+        pl.semaphore_wait(barrier, 2 + OWNERS - 1 + len(others))
+
+    @pl.when(jnp.logical_not(owner))
+    def _():
+        pl.semaphore_wait(barrier, 2 + OWNERS)
+
+    for i, (mine, theirs, side) in enumerate(
+        ((0, OWNERS - 1, left), (OWNERS - 1, 0, right))
+    ):
+        edge = edge_send.at[pl.ds(i * SUBS, SUBS)]
+        pltpu.make_async_remote_copy(
+            src_ref=edge,
+            dst_ref=slot(edge_far, place, SUBS, SUBS),
+            send_sem=edge_ssem,
+            recv_sem=far_rsem,
+            device_id={"solve": base + theirs, "cross": side},
+            device_id_type=MESH,
+        ).start()
+
+        @pl.when(place != mine)
+        def _():
+            pltpu.make_async_remote_copy(
+                src_ref=edge,
+                dst_ref=slot(edge_own, place, SUBS, SUBS),
+                send_sem=edge_ssem,
+                recv_sem=own_rsem,
+                device_id={"solve": base + mine},
+                device_id_type=MESH,
+            ).start()
+
+        @pl.when(place == mine)
+        def _():
+            edge_own[pl.ds(mine * SUBS, SUBS), :] = edge_send[pl.ds(i * SUBS, SUBS), :]
 
     zero = jnp.zeros((SUBS, LANES), jnp.float32)
     for block in range(4):
@@ -217,8 +270,6 @@
         start = (plane * 2 + i // SUBS) * SUBS * SUBS + i % SUBS
         return ref[pl.ds(start, SUBS, stride=SUBS), :]
 
-    loads_in[2].wait()
-    loads_in[3].wait()
     backs = []
     level = []
     back = []
@@ -261,105 +312,77 @@
             owns.append([pair[1] for pair in pairs])
         return level[0], owns
 
-    def slot(ref, index, rows, used, skip=0):
-        return ref.at[pl.ds(pl.multiple_of(index * rows, rows) + skip, used)]
-
     loads, _ = climb_loads()
     for j, value in enumerate(loads + element):
         part_send[pl.ds(j, SUBS, stride=SLOT), :] = value
 
-    @pl.when(owner)
-    def _():
-        pl.semaphore_wait(barrier, 2 + OWNERS - 1 + len(others))
-
-    @pl.when(jnp.logical_not(owner))
-    def _():
-        pl.semaphore_wait(barrier, 2 + OWNERS)
-
-    edge_copies = [
-        pltpu.make_async_remote_copy(
-            src_ref=edge_send.at[i],
-            dst_ref=edge_recv.at[i],
-            send_sem=edge_ssem.at[i],
-            recv_sem=edge_rsem.at[i],
-            device_id={"cross": side},
-            device_id_type=MESH,
-        )
-        for i, side in enumerate((left, right))
-    ]
-    for copy in edge_copies:
-        copy.start()
-
-    def part_copy(mate, skip, used):
-        return pltpu.make_async_remote_copy(
-            src_ref=slot(part_send, mate, SLOT, used, skip),
-            dst_ref=slot(part_recv, place, SLOT, used, skip),
-            send_sem=part_ssem,
-            recv_sem=part_rsem,
-            device_id={"solve": base + mate},
-            device_id_type=MESH,
-        )
-
     for mate in owners:
-        outer = (mate == 0) | (mate == OWNERS - 1)
-
-        @pl.when(outer & (mate != place))
-        def _():
-            part_copy(mate, LOADS, USED - LOADS).start()
-
-        @pl.when(jnp.logical_not(outer) & (mate != place))
-        def _():
-            part_copy(mate, 0, USED).start()
-
-    @pl.when(owner)
-    def _():
-        here = pl.ds(pl.multiple_of(place * SLOT, SLOT), USED)
-        part_recv[here, :] = part_send[here, :]
-
-    for i in (0, 1):
-        edge_copies[i].wait_recv()
-    for column, own, got, inside in (
-        (0, edges[0], edge_recv[1], cross > 0),
-        (SUBS - 1, edges[1], edge_recv[0], cross < n_cross - 1),
-    ):
-        got = jnp.where(inside, got, 0.0)
-        flux = 0.5 * spin(own + got, -4) * (got - own)
-        at = 0 if column == 0 else LANES - 1
-        for j in range(4):
-            where = pl.ds((j * SUBS + column) * SUBS, SUBS)
-            source[where, :] += jnp.where(lane == at, spin(flux, at - j), 0.0)
-
-    loads, owns = climb_loads()
-    for j in range(LOADS):
-        late_send[pl.ds(j, 1), :] = loads[j][0:1, :]
-        late_send[pl.ds(LOADS + j, 1), :] = loads[j][SUBS - 1 : SUBS, :]
-    for i, mate in enumerate((0, OWNERS - 1)):
-        ready = pl.ds(i * LOADS, LOADS)
-
-        @pl.when(place != mate)
+
+        @pl.when(mate != place)
         def _():
             pltpu.make_async_remote_copy(
-                src_ref=late_send.at[ready],
-                dst_ref=slot(part_recv, place, SLOT, LOADS),
+                src_ref=slot(part_send, mate, SLOT, USED),
+                dst_ref=slot(part_recv, place, SLOT, USED),
                 send_sem=part_ssem,
                 recv_sem=part_rsem,
                 device_id={"solve": base + mate},
                 device_id_type=MESH,
             ).start()
 
-        @pl.when(place == mate)
-        def _():
-            part_recv[pl.ds(mate * SLOT, LOADS), :] = late_send[ready, :]
+    @pl.when(owner)
+    def _():
+        here = pl.ds(pl.multiple_of(place * SLOT, SLOT), USED)
+        part_recv[here, :] = part_send[here, :]
 
     def climb(left_fields, right_fields):
         element, way = merge(left_fields[LOADS:], right_fields[LOADS:])
         loads, value = merge_loads(way, left_fields[:LOADS], right_fields[:LOADS])
         return loads + element, way, value
 
+    def wait_for(ref, rows, sem):
+        part = ref.at[pl.ds(0, rows)]
+        pltpu.make_async_copy(part, part, sem).wait()
+
+    @pl.when(outer)
+    def _():
+        wait_for(edge_own, (GROUP - 1) * SUBS, own_rsem)
+        wait_for(edge_far, GROUP * SUBS, far_rsem)
+        inside = jnp.where(place == 0, cross > 0, cross < n_cross - 1)
+        for mate in range(GROUP):
+            where = pl.ds(mate * SUBS, SUBS)
+            own = edge_own[where, :]
+            far = jnp.where(inside, edge_far[where, :], 0.0)
+            flux_send[where, :] = 0.5 * spin(own + far, -4) * (far - own)
+        flipped[pl.ds(0, 32), :] = edge_own[...].T[:32]
+        flipped[pl.ds(32, 32), :] = flux_send[...].T[:32]
+        side1, side2, first1, first2, second = (
+            flipped[pl.ds(at, SUBS), :] for at in (32, 34, 8, 10, 12)
+        )
+        element, way = merge_leaf(
+            second, spin(second, -1), first1, first2, spin(first1, -1), spin(first2, -1)
+        )
+        loads, _ = merge_leaf_loads(way, (side1, side2), (spin(side1, -1), spin(side2, -1)))
+        fields = loads + element
+        for shift in (2, 4):
+            fields, _, _ = climb(fields, tuple(spin(v, -shift) for v in fields))
+        fields, _, _ = climb(fields, tuple(pltpu.roll(v, SUBS - 1, 0) for v in fields))
+        rows = [fields[j][0:1, :] for j in range(LOADS)]
+        rows.append(jnp.zeros((LANES - LOADS, LANES), jnp.float32))
+        flipped[...] = jnp.concatenate(rows, axis=0).T
+
     @pl.when(owner)
     def _():
-        everything = part_recv.at[pl.ds(0, (GROUP - 1) * USED)]
-        pltpu.make_async_copy(everything, everything, part_rsem).wait()
+        wait_for(part_recv, (GROUP - 1) * USED, part_rsem)
+
+        @pl.when(outer)
+        def _():
+            for half in (0, 1):
+                got = flipped[pl.ds(half * SUBS * SUBS, SUBS, stride=SUBS), :]
+                for j in range(LOADS):
+                    rows = pl.ds(half * SUBS * SLOT + j, SUBS, stride=SLOT)
+                    start_lane = jnp.where(lane == 0, spin(got, -j), 0.0)
+                    end_lane = jnp.where(lane == LANES - 1, spin(got, -1 - j), 0.0)
+                    part_recv[rows, :] += jnp.where(place == 0, start_lane, end_lane)
 
         evens, odds = (
             tuple(part_recv[pl.ds(at + j, SUBS, stride=2 * SLOT), :] for j in range(USED))
@@ -389,6 +412,22 @@
             copy.start()
         here = pl.ds(pl.multiple_of(group * SLOT, SLOT), USED)
         line_recv[here, :] = line_send[pl.ds(0, USED), :]
+
+        for i, column in enumerate((0, OWNERS - 1)):
+
+            @pl.when(place == column)
+            def _():
+                for mate in mates:
+                    pltpu.make_async_remote_copy(
+                        src_ref=slot(flux_send, mate, SUBS, SUBS),
+                        dst_ref=flux_recv.at[pl.ds(i * SUBS, SUBS)],
+                        send_sem=flux_ssem,
+                        recv_sem=flux_rsem,
+                        device_id={"solve": base + mate},
+                        device_id_type=MESH,
+                    ).start()
+                flux_recv[pl.ds(i * SUBS, SUBS), :] = flux_send[pl.ds(column * SUBS, SUBS), :]
+
         everything = line_recv.at[pl.ds(0, (groups - 1) * USED)]
         pltpu.make_async_copy(everything, everything, line_rsem).wait()
 
@@ -449,9 +488,20 @@
         here = pl.ds(pl.multiple_of(place * LOADS, LOADS), LOADS)
         node_recv[here, :] = node_send[here, :]
 
-    def wait_for(ref, rows, sem):
-        part = ref.at[pl.ds(0, rows)]
-        pltpu.make_async_copy(part, part, sem).wait()
+    @pl.when(outer)
+    def _():
+        wait_for(flux_recv, SUBS, flux_rsem)
+
+    @pl.when(jnp.logical_not(outer))
+    def _():
+        wait_for(flux_recv, 2 * SUBS, flux_rsem)
+
+    for i, (column, at) in enumerate(((0, 0), (SUBS - 1, LANES - 1))):
+        flux = flux_recv[pl.ds(i * SUBS, SUBS), :]
+        for j in range(4):
+            where = pl.ds((j * SUBS + column) * SUBS, SUBS)
+            source[where, :] += jnp.where(lane == at, spin(flux, at - j), 0.0)
+    _, owns = climb_loads()
 
     @pl.when(owner)
     def _():
@@ -475,8 +525,15 @@
             start = (plane * 2 + i // SUBS) * SUBS * SUBS + i % SUBS
             out_ref[pl.ds(start, SUBS, stride=SUBS), :] = nodes[i][plane]
 
-    for copy in edge_copies:
-        copy.wait_send()
+    @pl.when(outer)
+    def _():
+        wait_for(edge_own, 3 * SUBS, edge_ssem)
+        wait_for(flux_send, (GROUP - 1) * SUBS, flux_ssem)
+
+    @pl.when(jnp.logical_not(outer))
+    def _():
+        wait_for(edge_own, 4 * SUBS, edge_ssem)
+
     @pl.when(owner)
     def _():
         wait_for(part_send, (OWNERS - 1) * USED, part_ssem)
@@ -508,19 +565,25 @@
             vmem(FLAT, LANES),
             vmem(FLAT // 2, LANES),
             vmem(FLAT, LANES),
-            vmem(2, SUBS, LANES),
-            vmem(2, SUBS, LANES),
+            vmem(2 * SUBS, LANES),
+            vmem(GROUP * SUBS, LANES),
+            vmem(GROUP * SUBS, LANES),
+            vmem(GROUP * SUBS, LANES),
+            vmem(2 * SUBS, LANES),
+            vmem(LANES, LANES),
             vmem(OWNERS * SLOT, LANES),
             vmem(GROUP * SLOT, LANES),
-            vmem(2 * LOADS, LANES),
             vmem(SLOT, LANES),
             vmem(groups * SLOT, LANES),
             vmem(2, SUBS, LANES),
             vmem(GROUP * LOADS, LANES),
             vmem(OWNERS * LOADS, LANES),
             dma((4,)),
-            dma((2,)),
-            dma((2,)),
+            dma,
+            dma,
+            dma,
+            dma,
+            dma,
             dma,
             dma,
             dma,

time: 28.1 us -> 27 us (0.961)
  Pallas kernels: 27.3 us -> 26.2 us
    pallas_call x1, Pallas kernels: 27.3 us -> 26.2 us  [per_device(): pl.pallas_call(functools.partial(kernel, groups), out_shape=jax.ShapeDtyp...]
where the time goes in v1:
time: 27 us; the launch traced here: 26.8 us
  Pallas kernels  26.2 us (97%)
  local copies, waits for them, and re-layouts  0.66 us (2%)
    pallas_call x1, Pallas kernels, per_device(): pl.pallas_call(functools.partial(kernel, groups), out_shape=jax.ShapeDtyp...  26.2 us
    unnamed x1, local copies, waits for them, and re-layouts  0.66 us

profile of v1, /device:TPU:1, one launch (start us, length us, event | category | flops | bytes accessed | tf_op | source)
XLA Modules:
  0.0 26.8 jit_solution(5136925123090241163)
XLA Ops:
  0.0 26.2 %line_step.1 = f32[256,128]{1,0:T(8,128)S(1)} custom-call(f32[256,128]{1,0:T(8,128)} %bitcast.26, f32[256,128]{1,0:T(8,128)} %bitcast.27, f32[256,128]{1,0:T(8,128)} %bitcast.28, f32[128,128]{1,0:T(8,128)} %bitcast.29), custom_call_target="tpu_custom_call" | custom-call | flops 4000000 | bytes 600000 | tf_op jit(solution)/shard_map/line_step/pallas_call | solution.py:557
  26.2 0.7 %copy.6 = f32[2,16,1024]{2,1,0:T(8,128)} copy(f32[2,16,1024]{2,1,0:T(8,128)S(1)} %bitcast.25) | data formatting | bytes 262144

commit v2 on v1

--- a/solution.py
+++ b/solution.py
@@ -198,8 +198,9 @@
     def tile(ref, block, column):
         return ref[pl.ds((block * SUBS + column) * SUBS, SUBS), :]
 
-    def slot(ref, index, rows, used, skip=0):
-        return ref.at[pl.ds(pl.multiple_of(index * rows, rows) + skip, used)]
+    def slot(ref, index, rows, used):
+        start = index * rows if isinstance(index, int) else pl.multiple_of(index * rows, rows)
+        return ref.at[pl.ds(start, used)]
 
     for copy in loads_in:
         copy.wait()
@@ -472,19 +473,19 @@
             )
         for j, value in enumerate(before + inner + inner + after):
             node_send[pl.ds(j, SUBS, stride=2 * LOADS), :] = value
-        node_copies = [
-            pltpu.make_async_remote_copy(
-                src_ref=slot(node_send, mate, LOADS, LOADS),
-                dst_ref=slot(node_recv, place, LOADS, LOADS),
-                send_sem=node_ssem,
-                recv_sem=node_rsem,
-                device_id={"solve": base + mate},
-                device_id_type=MESH,
-            )
-            for mate in mates
-        ]
-        for copy in node_copies:
-            copy.start()
+        for mate in [1, 0] + list(range(2, GROUP)):
+
+            @pl.when(place != mate)
+            def _():
+                pltpu.make_async_remote_copy(
+                    src_ref=slot(node_send, mate, LOADS, LOADS),
+                    dst_ref=slot(node_recv, place, LOADS, LOADS),
+                    send_sem=node_ssem,
+                    recv_sem=node_rsem,
+                    device_id={"solve": base + mate},
+                    device_id_type=MESH,
+                ).start()
+
         here = pl.ds(pl.multiple_of(place * LOADS, LOADS), LOADS)
         node_recv[here, :] = node_send[here, :]
 

time: 27 us -> 26.6 us (0.985)
  Pallas kernels: 26.2 us -> 25.8 us
    pallas_call x1, Pallas kernels: 26.2 us -> 25.8 us  [per_device(): pl.pallas_call(functools.partial(kernel, groups), out_shape=jax.ShapeDtyp...]
where the time goes in v2:
time: 26.6 us; the launch traced here: 26.5 us
  Pallas kernels  25.8 us (97%)
  local copies, waits for them, and re-layouts  0.66 us (2%)
    pallas_call x1, Pallas kernels, per_device(): pl.pallas_call(functools.partial(kernel, groups), out_shape=jax.ShapeDtyp...  25.8 us
    unnamed x1, local copies, waits for them, and re-layouts  0.66 us

profile of v2, /device:TPU:1, one launch (start us, length us, event | category | flops | bytes accessed | tf_op | source)
XLA Modules:
  0.0 26.5 jit_solution(16479803339834888887)
XLA Ops:
  0.0 25.8 %line_step.1 = f32[256,128]{1,0:T(8,128)S(1)} custom-call(f32[256,128]{1,0:T(8,128)} %bitcast.26, f32[256,128]{1,0:T(8,128)} %bitcast.27, f32[256,128]{1,0:T(8,128)} %bitcast.28, f32[128,128]{1,0:T(8,128)} %bitcast.29), custom_call_target="tpu_custom_call" | custom-call | flops 4000000 | bytes 600000 | tf_op jit(solution)/shard_map/line_step/pallas_call | solution.py:558
  25.8 0.7 %copy.6 = f32[2,16,1024]{2,1,0:T(8,128)} copy(f32[2,16,1024]{2,1,0:T(8,128)S(1)} %bitcast.25) | data formatting | bytes 262144

commit v3 on v1

v3 whole, which is shorter than its diff:
```python
import jax
import jax.numpy as jnp
from jax import lax
from jax.experimental import pallas as pl
from jax.experimental.pallas import tpu as pltpu
from jax.sharding import PartitionSpec as P

MESH = pl.DeviceIdType.MESH
ROWS, SUBS, LANES = 16, 8, 128
GROUP, OWNERS, PARTS = 16, 8, 64
FIRST, LAST = 0, 49
LOADS, USED, SLOT = 4, 14, 16
FLAT = 2 * ROWS * SUBS


def inverse(coupling, first, second):
    scale = 1.0 / (coupling * (first + second) + first * second)
    return (coupling + second) * scale, coupling * scale, (coupling + first) * scale


def merge(left, right):
    ea1, ea2, sa, n11, n12, n21, n22, ec1, ec2, sc = left
    fa1, fa2, fs, m11, m12, m21, m22, fc1, fc2, gs = right
    eb1, eb2, sb = ec1 + fa1, ec2 + fa2, sc + fs
    r1 = eb1 + ((n11 + n21) + (m11 + m12))
    r2 = eb2 + ((n12 + n22) + (m21 + m22))
    i11, i12, i22 = inverse(sb, r1, r2)
    g11, g12 = n11 * i11 + n12 * i12, n11 * i12 + n12 * i22
    g21, g22 = n21 * i11 + n22 * i12, n21 * i12 + n22 * i22
    h11, h12 = i11 * m11 + i12 * m21, i11 * m12 + i12 * m22
    h21, h22 = i12 * m11 + i22 * m21, i12 * m12 + i22 * m22
    joined = (
        ea1 + (g11 * eb1 + g12 * eb2),
        ea2 + (g21 * eb1 + g22 * eb2),
        sa + (g11 * n21 + g12 * n22),
        g11 * m11 + g12 * m21,
        g11 * m12 + g12 * m22,
        g21 * m11 + g22 * m21,
        g21 * m12 + g22 * m22,
        fc1 + (h11 * eb1 + h21 * eb2),
        fc2 + (h12 * eb1 + h22 * eb2),
        gs + (m11 * h12 + m21 * h22),
    )
    return joined, (i11, i12, i22, g11, g12, g21, g22, h11, h12, h21, h22)


def merge_leaf(sa, sb, n1, n2, m1, m2):
    r1, r2 = 1.0 + (n1 + m1), 1.0 + (n2 + m2)
    i11, i12, i22 = inverse(sb, r1, r2)
    g11, g12, g21, g22 = n1 * i11, n1 * i12, n2 * i12, n2 * i22
    h11, h12, h21, h22 = i11 * m1, i12 * m2, i12 * m1, i22 * m2
    joined = (
        1.0 + (g11 + g12),
        1.0 + (g21 + g22),
        sa + g12 * n2,
        g11 * m1,
        g12 * m2,
        g21 * m1,
        g22 * m2,
        h11 + h21,
        h12 + h22,
        m1 * h12,
    )
    return joined, (i11, i12, i22, g11, g12, g21, g22, h11, h12, h21, h22)


def merge_loads(back, left, right):
    i11, i12, i22, g11, g12, g21, g22, h11, h12, h21, h22 = back
    a1, a2, b1, b2 = left
    c1, c2, d1, d2 = right
    b1, b2 = b1 + c1, b2 + c2
    loads = (
        a1 + (g11 * b1 + g12 * b2),
        a2 + (g21 * b1 + g22 * b2),
        d1 + (h11 * b1 + h21 * b2),
        d2 + (h12 * b1 + h22 * b2),
    )
    return loads, (i11 * b1 + i12 * b2, i12 * b1 + i22 * b2)


def merge_leaf_loads(back, a, b):
    i11, i12, i22, g11, g12, g21, g22, h11, h12, h21, h22 = back
    a1, a2 = a
    b1, b2 = b
    loads = (
        a1 + (g11 * b1 + g12 * b2),
        a2 + (g21 * b1 + g22 * b2),
        h11 * b1 + h21 * b2,
        h12 * b1 + h22 * b2,
    )
    return loads, (i11 * b1 + i12 * b2, i12 * b1 + i22 * b2)


def middle(back, own, before, after):
    g11, g12, g21, g22, h11, h12, h21, h22 = back[3:]
    a1, a2 = before
    c1, c2 = after
    return (
        own[0] + ((g11 * a1 + g21 * a2) + (h11 * c1 + h12 * c2)),
        own[1] + ((g12 * a1 + g22 * a2) + (h21 * c1 + h22 * c2)),
    )


def kernel(
    temp_hbm,
    face_hbm,
    diff_hbm,
    sheet_hbm,
    out_ref,
    temp,
    face,
    diff,
    sheet,
    source,
    edge_send,
    edge_own,
    edge_far,
    flux_send,
    flux_recv,
    flipped,
    lined,
    part_send,
    part_recv,
    extra,
    node_send,
    node_recv,
    in_sem,
    edge_ssem,
    own_rsem,
    far_rsem,
    flux_ssem,
    flux_rsem,
    part_ssem,
    part_rsem,
    node_ssem,
    node_rsem,
):
    solve = lax.axis_index("solve")
    cross = lax.axis_index("cross")
    n_cross = lax.axis_size("cross")
    place = lax.rem(solve, GROUP)
    group = lax.div(solve, GROUP)

    loads_in = [
        pltpu.make_async_copy(src, dst, in_sem.at[i])
        for i, (src, dst) in enumerate(
            ((temp_hbm, temp), (diff_hbm, diff), (face_hbm, face), (sheet_hbm, sheet))
        )
    ]
    for copy in loads_in:
        copy.start()

    owner = place < 2
    column_row = group * 2 + place
    outer = (solve == FIRST) | (solve == LAST)
    rows_of = [lax.rem(solve + step, OWNERS) for step in range(OWNERS)]

    def device_of(index):
        return lax.div(index, 2) * GROUP + lax.rem(index, 2)

    right = lax.rem(cross + 1, n_cross)
    left = lax.rem(cross + n_cross - 1, n_cross)

    barrier = pltpu.get_barrier_semaphore()
    for column, side in ((FIRST, left), (LAST, right)):

        @pl.when(solve == column)
        def _():
            def greet(index, _):
                pl.semaphore_signal(
                    barrier,
                    1,
                    device_id={"solve": index, "cross": side},
                    device_id_type=MESH,
                )
                return 0

            lax.fori_loop(0, PARTS, greet, 0)

    @pl.when(owner)
    def _():
        def greet(step, _):
            pl.semaphore_signal(
                barrier,
                1,
                device_id={"solve": lax.rem(solve + step, PARTS)},
                device_id_type=MESH,
            )
            return 0

        lax.fori_loop(1, PARTS, greet, 0)
        extra[...] = jnp.zeros((PARTS * LOADS, LANES), jnp.float32)

    lane = lax.broadcasted_iota(jnp.int32, (SUBS, LANES), 1)
    sub = lax.broadcasted_iota(jnp.int32, (SUBS, LANES), 0)

    def spin(value, shift):
        return pltpu.roll(value, shift % LANES, 1)

    def tile(ref, block, column):
        return ref[pl.ds((block * SUBS + column) * SUBS, SUBS), :]

    def slot(ref, index, rows, used):
        start = index * rows if isinstance(index, int) else pl.multiple_of(index * rows, rows)
        return ref.at[pl.ds(start, used)]

    for copy in loads_in:
        copy.wait()
    tracks = [(ref, j) for ref in (temp, diff, face) for j in range(4)]
    tracks += [(sheet, 0), (sheet, 1)]
    for i, (column, shift) in enumerate(((0, 0), (SUBS - 1, 1))):
        packed = jnp.zeros((SUBS, LANES), jnp.float32)
        for j, (ref, block) in enumerate(tracks):
            packed = jnp.where(lane == j, spin(tile(ref, block, column), j + shift), packed)
        edge_send[pl.ds(i * SUBS, SUBS), :] = packed

    @pl.when(owner)
    def _():
        pl.semaphore_wait(barrier, 2 + OWNERS - 1)

    @pl.when(jnp.logical_not(owner))
    def _():
        pl.semaphore_wait(barrier, 2 + OWNERS)

    for i, (mine, theirs, side) in enumerate(
        ((FIRST, LAST, left), (LAST, FIRST, right))
    ):
        edge = edge_send.at[pl.ds(i * SUBS, SUBS)]
        pltpu.make_async_remote_copy(
            src_ref=edge,
            dst_ref=slot(edge_far, solve, SUBS, SUBS),
            send_sem=edge_ssem,
            recv_sem=far_rsem,
            device_id={"solve": theirs, "cross": side},
            device_id_type=MESH,
        ).start()

        @pl.when(solve != mine)
        def _():
            pltpu.make_async_remote_copy(
                src_ref=edge,
                dst_ref=slot(edge_own, solve, SUBS, SUBS),
                send_sem=edge_ssem,
                recv_sem=own_rsem,
                device_id={"solve": mine},
                device_id_type=MESH,
            ).start()

        @pl.when(solve == mine)
        def _():
            edge_own[pl.ds(mine * SUBS, SUBS), :] = edge_send[pl.ds(i * SUBS, SUBS), :]

    zero = jnp.zeros((SUBS, LANES), jnp.float32)
    for block in range(4):
        heat = [tile(temp, block, t) for t in range(SUBS)]
        cond = [tile(diff, block, t) for t in range(SUBS)]
        heat_turned = [spin(v, -1) for v in heat] + [zero]
        cond_turned = [spin(v, -1) for v in cond] + [zero]
        last = lane == LANES - 1
        before = zero
        for t in range(SUBS):
            next_heat = jnp.where(last, heat_turned[t + 1], heat_turned[t])
            next_cond = jnp.where(last, cond_turned[t + 1], cond_turned[t])
            flux = 0.5 * (cond[t] + next_cond) * (next_heat - heat[t])
            if t == SUBS - 1:
                flux = jnp.where(last, 0.0, flux)
            turned = spin(flux, 1)
            previous = jnp.where(lane == 0, before, turned)
            before = turned
            source[pl.ds((block * SUBS + t) * SUBS, SUBS), :] = heat[t] + flux - previous

    def row(ref, plane, i):
        start = (plane * 2 + i // SUBS) * SUBS * SUBS + i % SUBS
        return ref[pl.ds(start, SUBS, stride=SUBS), :]

    backs = []
    level = []
    back = []
    for m in range(ROWS // 2):
        element, way = merge_leaf(
            row(sheet, 0, 2 * m),
            row(sheet, 0, 2 * m + 1),
            row(face, 0, 2 * m),
            row(face, 1, 2 * m),
            row(face, 0, 2 * m + 1),
            row(face, 1, 2 * m + 1),
        )
        level.append(element)
        back.append(way)
    backs.append(back)
    while len(level) > 1:
        pairs = [merge(level[2 * m], level[2 * m + 1]) for m in range(len(level) // 2)]
        level = [pair[0] for pair in pairs]
        backs.append([pair[1] for pair in pairs])
    element = level[0]

    def climb_loads():
        owns = []
        level = []
        own = []
        for m in range(ROWS // 2):
            loads, value = merge_leaf_loads(
                backs[0][m],
                (row(source, 0, 2 * m), row(source, 1, 2 * m)),
                (row(source, 0, 2 * m + 1), row(source, 1, 2 * m + 1)),
            )
            level.append(loads)
            own.append(value)
        owns.append(own)
        for back in backs[1:]:
            pairs = [
                merge_loads(back[m], level[2 * m], level[2 * m + 1]) for m in range(len(back))
            ]
            level = [pair[0] for pair in pairs]
            owns.append([pair[1] for pair in pairs])
        return level[0], owns

    loads, _ = climb_loads()
    for j, value in enumerate(loads + element):
        part_send[pl.ds(j, SUBS, stride=SLOT), :] = value

    for index in rows_of:

        @pl.when(device_of(index) != solve)
        def _():
            pltpu.make_async_remote_copy(
                src_ref=slot(part_send, index, SLOT, USED),
                dst_ref=slot(part_recv, solve, SLOT, USED),
                send_sem=part_ssem,
                recv_sem=part_rsem,
                device_id={"solve": device_of(index)},
                device_id_type=MESH,
            ).start()

    @pl.when(owner)
    def _():
        here = pl.ds(pl.multiple_of(solve * SLOT, SLOT), USED)
        there = pl.ds(pl.multiple_of(column_row * SLOT, SLOT), USED)
        part_recv[here, :] = part_send[there, :]

    def climb(left_fields, right_fields):
        element, way = merge(left_fields[LOADS:], right_fields[LOADS:])
        loads, value = merge_loads(way, left_fields[:LOADS], right_fields[:LOADS])
        return loads + element, way, value

    def wait_for(ref, rows, sem):
        part = ref.at[pl.ds(0, rows)]
        pltpu.make_async_copy(part, part, sem).wait()

    def to_all(first, last, send):
        def one(n, _):
            part = lax.rem(lax.div(n, 2), 4) * GROUP + lax.div(n, 8) * 2 + lax.rem(n, 2)

            @pl.when(part != solve)
            def _():
                send(part)

            return 0

        lax.fori_loop(first, last, one, 0)

    def flux_to(i):
        def send(part):
            pltpu.make_async_remote_copy(
                src_ref=slot(flux_send, lax.div(part, GROUP), 4, 4),
                dst_ref=flux_recv.at[pl.ds(i * 4, 4)],
                send_sem=flux_ssem,
                recv_sem=flux_rsem,
                device_id={"solve": part},
                device_id_type=MESH,
            ).start()

        return send

    for i, (column, at, inside) in enumerate(
        ((FIRST, 0, cross > 0), (LAST, LANES - 1, cross < n_cross - 1))
    ):

        @pl.when(solve == column)
        def _():
            wait_for(edge_own, (PARTS - 1) * SUBS, own_rsem)
            wait_for(edge_far, PARTS * SUBS, far_rsem)
            for g in range(PARTS // GROUP):
                where = pl.ds(g * LANES, LANES)
                own = edge_own[where, :]
                far = jnp.where(inside, edge_far[where, :], 0.0)
                flux = 0.5 * spin(own + far, -4) * (far - own)
                flipped[pl.ds(0, SUBS), :] = flux.T[:SUBS]
                flipped[pl.ds(SUBS, 2 * SUBS), :] = own.T[: 2 * SUBS]
                flux_send[pl.ds(g * 4, 4), :] = flipped[pl.ds(0, 4), :]
                for f, row_at in enumerate((0, 2, 16, 18, 20)):
                    lined[pl.ds(f * SUBS + 2 * g, 2), :] = flipped[pl.ds(row_at, 2), :]
            side1, side2, first1, first2, second = (
                lined[pl.ds(f * SUBS, SUBS), :] for f in range(5)
            )
            element, way = merge_leaf(
                second, spin(second, -1), first1, first2, spin(first1, -1), spin(first2, -1)
            )
            loads, _ = merge_leaf_loads(
                way, (side1, side2), (spin(side1, -1), spin(side2, -1))
            )
            fields = loads + element
            for shift in (2, 4):
                fields, _, _ = climb(fields, tuple(spin(v, -shift) for v in fields))
            fields, _, _ = climb(fields, tuple(pltpu.roll(v, SUBS - 1, 0) for v in fields))
            rows = list(fields[:LOADS])
            rows.append(jnp.zeros((LANES - LOADS * SUBS, LANES), jnp.float32))
            flipped[...] = jnp.concatenate(rows, axis=0).T
            for half in (0, 1):
                got = flipped[pl.ds(half * SUBS * SUBS, SUBS, stride=SUBS), :]
                for g in range(PARTS // GROUP):
                    for j in range(LOADS):
                        moved = spin(got, at - j * SUBS - 2 * g)
                        at_rows = pl.ds(
                            (g * GROUP + half * SUBS) * LOADS + j, SUBS, stride=LOADS
                        )
                        extra[at_rows, :] = jnp.where(lane == at, moved, 0.0)
            to_all(0, 16, flux_to(i))
            flux_recv[pl.ds(i * 4, 4), :] = flux_send[pl.ds((column // GROUP) * 4, 4), :]

    @pl.when(owner)
    def _():
        wait_for(part_recv, (PARTS - 1) * USED, part_rsem)

        level = []
        for k in range(SUBS):
            loads = tuple(
                part_recv[pl.ds(k * SLOT + j, SUBS, stride=SUBS * SLOT), :]
                + extra[pl.ds(k * LOADS + j, SUBS, stride=SUBS * LOADS), :]
                for j in range(LOADS)
            )
            rest = tuple(
                part_recv[pl.ds(k * SLOT + j, SUBS, stride=SUBS * SLOT), :]
                for j in range(LOADS, USED)
            )
            level.append(loads + rest)
        steps = []
        while len(level) > 1:
            joined = [climb(level[2 * m], level[2 * m + 1]) for m in range(len(level) // 2)]
            steps.append([item[1:] for item in joined])
            level = [item[0] for item in joined]
        fields = level[0]
        trail = []
        for shift in (1, 2, 4):
            raised = tuple(pltpu.roll(v, SUBS - shift, 0) for v in fields)
            fields, way, value = climb(fields, raised)
            trail.append((way, value, shift))
        f1, f2, _, _, ea1, ea2, sa, n11, n12, n21, n22, _, _, _ = fields
        i11, i12, i22 = inverse(sa, ea1 + (n11 + n12), ea2 + (n21 + n22))
        before = (i11 * f1 + i12 * f2, i12 * f1 + i22 * f2)
        after = (zero, zero)

        for way, value, shift in reversed(trail):
            inner = middle(way, value, before, after)
            first = (sub & shift) == 0
            before = tuple(
                jnp.where(first, b, pltpu.roll(v, shift, 0)) for b, v in zip(before, inner)
            )
            after = tuple(
                jnp.where(first, v, pltpu.roll(a, shift, 0)) for v, a in zip(inner, after)
            )
        nodes = [before, after]
        for step in reversed(steps):
            finer = []
            for m, (way, value) in enumerate(step):
                finer += [nodes[m], middle(way, value, nodes[m], nodes[m + 1])]
            nodes = finer + [nodes[-1]]
        for k in range(SUBS):
            for j, value in enumerate(nodes[k] + nodes[k + 1]):
                node_send[pl.ds(k * LOADS + j, SUBS, stride=SUBS * LOADS), :] = value

        def values_to(part):
            pltpu.make_async_remote_copy(
                src_ref=slot(node_send, part, LOADS, LOADS),
                dst_ref=slot(node_recv, column_row, LOADS, LOADS),
                send_sem=node_ssem,
                recv_sem=node_rsem,
                device_id={"solve": part},
                device_id_type=MESH,
            ).start()

        to_all(0, PARTS, values_to)
        here = pl.ds(pl.multiple_of(column_row * LOADS, LOADS), LOADS)
        there = pl.ds(pl.multiple_of(solve * LOADS, LOADS), LOADS)
        node_recv[here, :] = node_send[there, :]

    for i, column in enumerate((FIRST, LAST)):

        @pl.when(solve == column)
        def _():
            to_all(16, PARTS, flux_to(i))

    @pl.when(outer)
    def _():
        wait_for(flux_recv, 4, flux_rsem)

    @pl.when(jnp.logical_not(outer))
    def _():
        wait_for(flux_recv, 8, flux_rsem)

    flux = pltpu.roll(flux_recv[...], lax.rem(LANES - place * SUBS, LANES), 1)
    flux = jnp.concatenate([flux, jnp.zeros((LANES - SUBS, LANES), jnp.float32)], axis=0).T
    flux = flux[:SUBS]
    for i, (column, at) in enumerate(((0, 0), (SUBS - 1, LANES - 1))):
        for j in range(4):
            where = pl.ds((j * SUBS + column) * SUBS, SUBS)
            source[where, :] += jnp.where(lane == at, spin(flux, at - j - 4 * i), 0.0)
    _, owns = climb_loads()

    @pl.when(owner)
    def _():
        wait_for(node_recv, (OWNERS - 1) * LOADS, node_rsem)

    @pl.when(jnp.logical_not(owner))
    def _():
        wait_for(node_recv, OWNERS * LOADS, node_rsem)

    values = [node_recv[pl.ds(j, SUBS, stride=LOADS), :] for j in range(LOADS)]
    ends = [tuple(values[:2]), tuple(values[2:])]

    nodes = ends
    for back, own in zip(reversed(backs), reversed(owns)):
        finer = []
        for m in range(len(back)):
            finer += [nodes[m], middle(back[m], own[m], nodes[m], nodes[m + 1])]
        nodes = finer + [nodes[-1]]
    for i in range(ROWS):
        for plane in (0, 1):
            start = (plane * 2 + i // SUBS) * SUBS * SUBS + i % SUBS
            out_ref[pl.ds(start, SUBS, stride=SUBS), :] = nodes[i][plane]

    @pl.when(outer)
    def _():
        wait_for(edge_own, 3 * SUBS, edge_ssem)
        wait_for(node_send, (PARTS - 1) * 4, flux_ssem)

    @pl.when(jnp.logical_not(outer))
    def _():
        wait_for(edge_own, 4 * SUBS, edge_ssem)

    @pl.when(owner)
    def _():
        wait_for(part_send, (OWNERS - 1) * USED, part_ssem)
        wait_for(node_send, (PARTS - 1) * LOADS, node_ssem)

    @pl.when(jnp.logical_not(owner))
    def _():
        wait_for(part_send, OWNERS * USED, part_ssem)


def tiles(array):
    array = array.reshape(-1, ROWS // SUBS, SUBS, SUBS, LANES)
    return array.transpose(0, 1, 3, 2, 4).reshape(-1, LANES)


def per_device(temperature, transfer, diffusivity, exchange):
    vmem = lambda *shape: pltpu.VMEM(shape, jnp.float32)
    dma = pltpu.SemaphoreType.DMA
    out = pl.pallas_call(
        kernel,
        out_shape=jax.ShapeDtypeStruct((FLAT, LANES), jnp.float32),
        in_specs=[pl.BlockSpec(memory_space=pltpu.HBM)] * 4,
        out_specs=pl.BlockSpec(memory_space=pltpu.VMEM),
        scratch_shapes=[
            vmem(FLAT, LANES),
            vmem(FLAT, LANES),
            vmem(FLAT, LANES),
            vmem(FLAT // 2, LANES),
            vmem(FLAT, LANES),
            vmem(2 * SUBS, LANES),
            vmem(PARTS * SUBS, LANES),
            vmem(PARTS * SUBS, LANES),
            vmem(2 * SUBS, LANES),
            vmem(SUBS, LANES),
            vmem(LANES, LANES),
            vmem(5 * SUBS, LANES),
            vmem(OWNERS * SLOT, LANES),
            vmem(PARTS * SLOT, LANES),
            vmem(PARTS * LOADS, LANES),
            vmem(PARTS * LOADS, LANES),
            vmem(OWNERS * LOADS, LANES),
            dma((4,)),
            dma,
            dma,
            dma,
            dma,
            dma,
            dma,
            dma,
            dma,
            dma,
        ],
        compiler_params=pltpu.CompilerParams(
            collective_id=0, has_side_effects=True, vmem_limit_bytes=16 * 1024 * 1024
        ),
        cost_estimate=pl.CostEstimate(
            flops=4_000_000, bytes_accessed=600_000, transcendentals=0
        ),
        name="line_step",
    )(
        *(
            pltpu.with_memory_space_constraint(tiles(array), pltpu.HBM)
            for array in (temperature, transfer, diffusivity, exchange)
        )
    )
    out = out.reshape(2, ROWS // SUBS, SUBS, SUBS, LANES).transpose(0, 1, 3, 2, 4)
    return out.reshape(2, ROWS, SUBS * LANES)


def solution(mesh):
    specs = (P(None, "solve", "cross"),) * 3 + (P("solve", "cross"),)
    return jax.shard_map(
        per_device,
        mesh=mesh,
        in_specs=specs,
        out_specs=P(None, "solve", "cross"),
        check_vma=False,
    )
```

time: 27 us -> 26.4 us (0.978)
  Pallas kernels: 26.2 us -> 25.6 us
    pallas_call x1, Pallas kernels: 26.2 us -> 25.6 us  [per_device(): pl.pallas_call(kernel, out_shape=jax.ShapeDtypeStruct((FLAT, LANES), jnp....]
where the time goes in v3:
time: 26.4 us; the launch traced here: 26.3 us
  Pallas kernels  25.6 us (97%)
  local copies, waits for them, and re-layouts  0.66 us (2%)
    pallas_call x1, Pallas kernels, per_device(): pl.pallas_call(kernel, out_shape=jax.ShapeDtypeStruct((FLAT, LANES), jnp....  25.6 us
    unnamed x1, local copies, waits for them, and re-layouts  0.66 us

profile of v3, /device:TPU:1, one launch (start us, length us, event | category | flops | bytes accessed | tf_op | source)
XLA Modules:
  0.0 26.3 jit_solution(12362458894515492141)
XLA Ops:
  0.0 25.6 %line_step.1 = f32[256,128]{1,0:T(8,128)S(1)} custom-call(f32[256,128]{1,0:T(8,128)} %bitcast.26, f32[256,128]{1,0:T(8,128)} %bitcast.27, f32[256,128]{1,0:T(8,128)} %bitcast.28, f32[128,128]{1,0:T(8,128)} %bitcast.29), custom_call_target="tpu_custom_call" | custom-call | flops 4000000 | bytes 600000 | tf_op jit(solution)/shard_map/line_step/pallas_call | solution.py:559
  25.6 0.7 %copy.6 = f32[2,16,1024]{2,1,0:T(8,128)} copy(f32[2,16,1024]{2,1,0:T(8,128)S(1)} %bitcast.25) | data formatting | bytes 262144

commit v4 on v3

--- a/solution.py
+++ b/solution.py
@@ -117,8 +117,6 @@
     edge_far,
     flux_send,
     flux_recv,
-    flipped,
-    lined,
     part_send,
     part_recv,
     extra,
@@ -194,6 +192,8 @@
     lane = lax.broadcasted_iota(jnp.int32, (SUBS, LANES), 1)
     sub = lax.broadcasted_iota(jnp.int32, (SUBS, LANES), 0)
 
+    zero = jnp.zeros((SUBS, LANES), jnp.float32)
+
     def spin(value, shift):
         return pltpu.roll(value, shift % LANES, 1)
 
@@ -211,8 +211,12 @@
     for i, (column, shift) in enumerate(((0, 0), (SUBS - 1, 1))):
         packed = jnp.zeros((SUBS, LANES), jnp.float32)
         for j, (ref, block) in enumerate(tracks):
-            packed = jnp.where(lane == j, spin(tile(ref, block, column), j + shift), packed)
-        edge_send[pl.ds(i * SUBS, SUBS), :] = packed
+            at = j * SUBS
+            packed = jnp.where(lane == at, spin(tile(ref, block, column), at + shift), packed)
+        for step in (1, 2, 4):
+            packed = packed + spin(pltpu.roll(packed, SUBS - step, 0), step)
+        edge_send[pl.ds(i, 1), :] = packed[0:1, :]
+    flux_recv[pl.ds(4, 4), :] = zero[0:4, :]
 
     @pl.when(owner)
     def _():
@@ -225,10 +229,10 @@
     for i, (mine, theirs, side) in enumerate(
         ((FIRST, LAST, left), (LAST, FIRST, right))
     ):
-        edge = edge_send.at[pl.ds(i * SUBS, SUBS)]
+        edge = edge_send.at[pl.ds(i, 1)]
         pltpu.make_async_remote_copy(
             src_ref=edge,
-            dst_ref=slot(edge_far, solve, SUBS, SUBS),
+            dst_ref=slot(edge_far, solve, 1, 1),
             send_sem=edge_ssem,
             recv_sem=far_rsem,
             device_id={"solve": theirs, "cross": side},
@@ -239,7 +243,7 @@
         def _():
             pltpu.make_async_remote_copy(
                 src_ref=edge,
-                dst_ref=slot(edge_own, solve, SUBS, SUBS),
+                dst_ref=slot(edge_own, solve, 1, 1),
                 send_sem=edge_ssem,
                 recv_sem=own_rsem,
                 device_id={"solve": mine},
@@ -248,9 +252,8 @@
 
         @pl.when(solve == mine)
         def _():
-            edge_own[pl.ds(mine * SUBS, SUBS), :] = edge_send[pl.ds(i * SUBS, SUBS), :]
-
-    zero = jnp.zeros((SUBS, LANES), jnp.float32)
+            edge_own[pl.ds(mine, 1), :] = edge_send[pl.ds(i, 1), :]
+
     for block in range(4):
         heat = [tile(temp, block, t) for t in range(SUBS)]
         cond = [tile(diff, block, t) for t in range(SUBS)]
@@ -362,8 +365,8 @@
     def flux_to(i):
         def send(part):
             pltpu.make_async_remote_copy(
-                src_ref=slot(flux_send, lax.div(part, GROUP), 4, 4),
-                dst_ref=flux_recv.at[pl.ds(i * 4, 4)],
+                src_ref=slot(flux_send, lax.rem(part, SUBS), 2, 2),
+                dst_ref=flux_recv.at[pl.ds(i * 2, 2)],
                 send_sem=flux_ssem,
                 recv_sem=flux_rsem,
                 device_id={"solve": part},
@@ -372,51 +375,43 @@
 
         return send
 
+    def along(ref, at, inside=None):
+        value = zero
+        for a in range(SUBS):
+            part = spin(ref[pl.ds(a * SUBS, SUBS), :], a * ROWS - at)
+            value = jnp.where(lax.div(lane, ROWS) == a, part, value)
+        return value if inside is None else jnp.where(inside, value, 0.0)
+
     for i, (column, at, inside) in enumerate(
         ((FIRST, 0, cross > 0), (LAST, LANES - 1, cross < n_cross - 1))
     ):
 
         @pl.when(solve == column)
         def _():
-            wait_for(edge_own, (PARTS - 1) * SUBS, own_rsem)
-            wait_for(edge_far, PARTS * SUBS, far_rsem)
-            for g in range(PARTS // GROUP):
-                where = pl.ds(g * LANES, LANES)
-                own = edge_own[where, :]
-                far = jnp.where(inside, edge_far[where, :], 0.0)
-                flux = 0.5 * spin(own + far, -4) * (far - own)
-                flipped[pl.ds(0, SUBS), :] = flux.T[:SUBS]
-                flipped[pl.ds(SUBS, 2 * SUBS), :] = own.T[: 2 * SUBS]
-                flux_send[pl.ds(g * 4, 4), :] = flipped[pl.ds(0, 4), :]
-                for f, row_at in enumerate((0, 2, 16, 18, 20)):
-                    lined[pl.ds(f * SUBS + 2 * g, 2), :] = flipped[pl.ds(row_at, 2), :]
-            side1, side2, first1, first2, second = (
-                lined[pl.ds(f * SUBS, SUBS), :] for f in range(5)
-            )
+            wait_for(edge_own, PARTS - 1, own_rsem)
+            wait_for(edge_far, PARTS, far_rsem)
+            sides = []
+            for plane in (0, 1):
+                warm, cond = plane * ROWS, (2 + plane) * ROWS
+                total = along(edge_own, cond) + along(edge_far, cond, inside)
+                step = along(edge_far, warm, inside) - along(edge_own, warm)
+                sides.append(0.5 * total * step)
+                flux_send[pl.ds(plane, SUBS, stride=2), :] = sides[plane]
+            first1, first2, second = (along(edge_own, f * ROWS) for f in (4, 5, 6))
             element, way = merge_leaf(
                 second, spin(second, -1), first1, first2, spin(first1, -1), spin(first2, -1)
             )
-            loads, _ = merge_leaf_loads(
-                way, (side1, side2), (spin(side1, -1), spin(side2, -1))
-            )
+            loads, _ = merge_leaf_loads(way, sides, [spin(v, -1) for v in sides])
             fields = loads + element
-            for shift in (2, 4):
+            for shift in (2, 4, 8):
                 fields, _, _ = climb(fields, tuple(spin(v, -shift) for v in fields))
-            fields, _, _ = climb(fields, tuple(pltpu.roll(v, SUBS - 1, 0) for v in fields))
-            rows = list(fields[:LOADS])
-            rows.append(jnp.zeros((LANES - LOADS * SUBS, LANES), jnp.float32))
-            flipped[...] = jnp.concatenate(rows, axis=0).T
-            for half in (0, 1):
-                got = flipped[pl.ds(half * SUBS * SUBS, SUBS, stride=SUBS), :]
-                for g in range(PARTS // GROUP):
-                    for j in range(LOADS):
-                        moved = spin(got, at - j * SUBS - 2 * g)
-                        at_rows = pl.ds(
-                            (g * GROUP + half * SUBS) * LOADS + j, SUBS, stride=LOADS
-                        )
-                        extra[at_rows, :] = jnp.where(lane == at, moved, 0.0)
+            for a in range(SUBS):
+                for j in range(LOADS):
+                    at_rows = pl.ds(a * SUBS * LOADS + j, SUBS, stride=LOADS)
+                    moved = spin(fields[j], at - a * ROWS)
+                    extra[at_rows, :] = jnp.where(lane == at, moved, 0.0)
             to_all(0, 16, flux_to(i))
-            flux_recv[pl.ds(i * 4, 4), :] = flux_send[pl.ds((column // GROUP) * 4, 4), :]
+            flux_recv[pl.ds(i * 2, 2), :] = flux_send[pl.ds((column % SUBS) * 2, 2), :]
 
     @pl.when(owner)
     def _():
@@ -492,19 +487,21 @@
 
     @pl.when(outer)
     def _():
+        wait_for(flux_recv, 2, flux_rsem)
+
+    @pl.when(jnp.logical_not(outer))
+    def _():
         wait_for(flux_recv, 4, flux_rsem)
 
-    @pl.when(jnp.logical_not(outer))
-    def _():
-        wait_for(flux_recv, 8, flux_rsem)
-
-    flux = pltpu.roll(flux_recv[...], lax.rem(LANES - place * SUBS, LANES), 1)
+    shift = lax.rem(LANES - lax.div(solve, SUBS) * ROWS, LANES)
+    flux = pltpu.roll(flux_recv[...], shift, 1)
     flux = jnp.concatenate([flux, jnp.zeros((LANES - SUBS, LANES), jnp.float32)], axis=0).T
-    flux = flux[:SUBS]
     for i, (column, at) in enumerate(((0, 0), (SUBS - 1, LANES - 1))):
         for j in range(4):
             where = pl.ds((j * SUBS + column) * SUBS, SUBS)
-            source[where, :] += jnp.where(lane == at, spin(flux, at - j - 4 * i), 0.0)
+            part = flux[(j % 2) * SUBS : (j % 2 + 1) * SUBS]
+            moved = spin(part, at - 2 * i - j // 2)
+            source[where, :] += jnp.where(lane == at, moved, 0.0)
     _, owns = climb_loads()
 
     @pl.when(owner)
@@ -531,12 +528,12 @@
 
     @pl.when(outer)
     def _():
-        wait_for(edge_own, 3 * SUBS, edge_ssem)
-        wait_for(node_send, (PARTS - 1) * 4, flux_ssem)
+        wait_for(edge_own, 3, edge_ssem)
+        wait_for(node_send, (PARTS - 1) * 2, flux_ssem)
 
     @pl.when(jnp.logical_not(outer))
     def _():
-        wait_for(edge_own, 4 * SUBS, edge_ssem)
+        wait_for(edge_own, 4, edge_ssem)
 
     @pl.when(owner)
     def _():
@@ -567,13 +564,11 @@
             vmem(FLAT, LANES),
             vmem(FLAT // 2, LANES),
             vmem(FLAT, LANES),
-            vmem(2 * SUBS, LANES),
-            vmem(PARTS * SUBS, LANES),
-            vmem(PARTS * SUBS, LANES),
+            vmem(SUBS, LANES),
+            vmem(PARTS, LANES),
+            vmem(PARTS, LANES),
             vmem(2 * SUBS, LANES),
             vmem(SUBS, LANES),
-            vmem(LANES, LANES),
-            vmem(5 * SUBS, LANES),
             vmem(OWNERS * SLOT, LANES),
             vmem(PARTS * SLOT, LANES),
             vmem(PARTS * LOADS, LANES),

time: 26.4 us -> 25.2 us (0.955)
  Pallas kernels: 25.6 us -> 24.4 us
    pallas_call x1, Pallas kernels: 25.6 us -> 24.4 us  [per_device(): pl.pallas_call(kernel, out_shape=jax.ShapeDtypeStruct((FLAT, LANES), jnp....]
where the time goes in v4:
time: 25.2 us; the launch traced here: 25.1 us
  Pallas kernels  24.4 us (97%)
  local copies, waits for them, and re-layouts  0.66 us (3%)
    pallas_call x1, Pallas kernels, per_device(): pl.pallas_call(kernel, out_shape=jax.ShapeDtypeStruct((FLAT, LANES), jnp....  24.4 us
    unnamed x1, local copies, waits for them, and re-layouts  0.66 us

profile of v4, /device:TPU:1, one launch (start us, length us, event | category | flops | bytes accessed | tf_op | source)
XLA Modules:
  0.0 25.1 jit_solution(18054546021594384756)
XLA Ops:
  0.0 24.4 %line_step.1 = f32[256,128]{1,0:T(8,128)S(1)} custom-call(f32[256,128]{1,0:T(8,128)} %bitcast.26, f32[256,128]{1,0:T(8,128)} %bitcast.27, f32[256,128]{1,0:T(8,128)} %bitcast.28, f32[128,128]{1,0:T(8,128)} %bitcast.29), custom_call_target="tpu_custom_call" | custom-call | flops 4000000 | bytes 600000 | tf_op jit(solution)/shard_map/line_step/pallas_call | solution.py:556
  24.5 0.7 %copy.6 = f32[2,16,1024]{2,1,0:T(8,128)} copy(f32[2,16,1024]{2,1,0:T(8,128)S(1)} %bitcast.25) | data formatting | bytes 262144

commit v5 on v4

--- a/solution.py
+++ b/solution.py
@@ -1,3 +1,5 @@
+import functools
+
 import jax
 import jax.numpy as jnp
 from jax import lax
@@ -118,6 +120,7 @@
     flux_send,
     flux_recv,
     part_send,
+    late_send,
     part_recv,
     extra,
     node_send,
@@ -254,24 +257,6 @@
         def _():
             edge_own[pl.ds(mine, 1), :] = edge_send[pl.ds(i, 1), :]
 
-    for block in range(4):
-        heat = [tile(temp, block, t) for t in range(SUBS)]
-        cond = [tile(diff, block, t) for t in range(SUBS)]
-        heat_turned = [spin(v, -1) for v in heat] + [zero]
-        cond_turned = [spin(v, -1) for v in cond] + [zero]
-        last = lane == LANES - 1
-        before = zero
-        for t in range(SUBS):
-            next_heat = jnp.where(last, heat_turned[t + 1], heat_turned[t])
-            next_cond = jnp.where(last, cond_turned[t + 1], cond_turned[t])
-            flux = 0.5 * (cond[t] + next_cond) * (next_heat - heat[t])
-            if t == SUBS - 1:
-                flux = jnp.where(last, 0.0, flux)
-            turned = spin(flux, 1)
-            previous = jnp.where(lane == 0, before, turned)
-            before = turned
-            source[pl.ds((block * SUBS + t) * SUBS, SUBS), :] = heat[t] + flux - previous
-
     def row(ref, plane, i):
         start = (plane * 2 + i // SUBS) * SUBS * SUBS + i % SUBS
         return ref[pl.ds(start, SUBS, stride=SUBS), :]
@@ -297,6 +282,47 @@
         backs.append([pair[1] for pair in pairs])
     element = level[0]
 
+    def send_parts(ref, slot_rows, skip, rows):
+        def rows_at(ref, slot_rows, index):
+            start = pl.multiple_of(index * slot_rows, slot_rows) + skip % slot_rows
+            return ref.at[pl.ds(start, rows)]
+
+        for index in rows_of:
+
+            @pl.when(device_of(index) != solve)
+            def _():
+                pltpu.make_async_remote_copy(
+                    src_ref=rows_at(ref, slot_rows, index),
+                    dst_ref=rows_at(part_recv, SLOT, solve),
+                    send_sem=part_ssem,
+                    recv_sem=part_rsem,
+                    device_id={"solve": device_of(index)},
+                    device_id_type=MESH,
+                ).start()
+
+    for j, value in enumerate(element):
+        part_send[pl.ds(LOADS + j, SUBS, stride=SLOT), :] = value
+    send_parts(part_send, SLOT, LOADS, USED - LOADS)
+
+    for block in range(4):
+        heat = [tile(temp, block, t) for t in range(SUBS)]
+        cond = [tile(diff, block, t) for t in range(SUBS)]
+        heat_turned = [spin(v, -1) for v in heat] + [zero]
+        cond_turned = [spin(v, -1) for v in cond] + [zero]
+        last = lane == LANES - 1
+        before = zero
+        for t in range(SUBS):
+            next_heat = jnp.where(last, heat_turned[t + 1], heat_turned[t])
+            next_cond = jnp.where(last, cond_turned[t + 1], cond_turned[t])
+            flux = 0.5 * (cond[t] + next_cond) * (next_heat - heat[t])
+            if t == SUBS - 1:
+                flux = jnp.where(last, 0.0, flux)
+            turned = spin(flux, 1)
+            previous = jnp.where(lane == 0, before, turned)
+            before = turned
+            source[pl.ds((block * SUBS + t) * SUBS, SUBS), :] = heat[t] + flux - previous
+
+
     def climb_loads():
         owns = []
         level = []
@@ -319,27 +345,20 @@
         return level[0], owns
 
     loads, _ = climb_loads()
-    for j, value in enumerate(loads + element):
-        part_send[pl.ds(j, SUBS, stride=SLOT), :] = value
-
-    for index in rows_of:
-
-        @pl.when(device_of(index) != solve)
-        def _():
-            pltpu.make_async_remote_copy(
-                src_ref=slot(part_send, index, SLOT, USED),
-                dst_ref=slot(part_recv, solve, SLOT, USED),
-                send_sem=part_ssem,
-                recv_sem=part_rsem,
-                device_id={"solve": device_of(index)},
-                device_id_type=MESH,
-            ).start()
+    for j, value in enumerate(loads):
+        late_send[pl.ds(j, SUBS, stride=LOADS), :] = value
+
+    send_parts(late_send, LOADS, 0, LOADS)
 
     @pl.when(owner)
     def _():
-        here = pl.ds(pl.multiple_of(solve * SLOT, SLOT), USED)
-        there = pl.ds(pl.multiple_of(column_row * SLOT, SLOT), USED)
-        part_recv[here, :] = part_send[there, :]
+        here = pl.multiple_of(solve * SLOT, SLOT)
+        there = pl.multiple_of(column_row * SLOT, SLOT) + LOADS
+        late = pl.ds(pl.multiple_of(column_row * LOADS, LOADS), LOADS)
+        part_recv[pl.ds(here, LOADS), :] = late_send[late, :]
+        part_recv[pl.ds(here + LOADS, USED - LOADS), :] = part_send[
+            pl.ds(there, USED - LOADS), :
+        ]
 
     def climb(left_fields, right_fields):
         element, way = merge(left_fields[LOADS:], right_fields[LOADS:])
@@ -474,7 +493,12 @@
                 device_id_type=MESH,
             ).start()
 
-        to_all(0, PARTS, values_to)
+        for n in range(PARTS):
+            part = (n // 2) % 4 * GROUP + n // 8 * 2 + n % 2
+            if n < OWNERS:
+                pl.when(solve != part)(functools.partial(values_to, part))
+            else:
+                values_to(part)
         here = pl.ds(pl.multiple_of(column_row * LOADS, LOADS), LOADS)
         there = pl.ds(pl.multiple_of(solve * LOADS, LOADS), LOADS)
         node_recv[here, :] = node_send[there, :]
@@ -570,6 +594,7 @@
             vmem(2 * SUBS, LANES),
             vmem(SUBS, LANES),
             vmem(OWNERS * SLOT, LANES),
+            vmem(OWNERS * LOADS, LANES),
             vmem(PARTS * SLOT, LANES),
             vmem(PARTS * LOADS, LANES),
             vmem(PARTS * LOADS, LANES),

time: 25.2 us -> 25.1 us (level)
  no operation moved by 1% of the time
where the time goes in v5:
time: 25.1 us; the launch traced here: 25 us
  Pallas kernels  24.3 us (97%)
  local copies, waits for them, and re-layouts  0.66 us (3%)
    pallas_call x1, Pallas kernels, per_device(): pl.pallas_call(kernel, out_shape=jax.ShapeDtypeStruct((FLAT, LANES), jnp....  24.3 us
    unnamed x1, local copies, waits for them, and re-layouts  0.66 us

profile of v5, /device:TPU:1, one launch (start us, length us, event | category | flops | bytes accessed | tf_op | source)
XLA Modules:
  0.0 25.0 jit_solution(13211031566944495960)
XLA Ops:
  0.0 24.3 %line_step.1 = f32[256,128]{1,0:T(8,128)S(1)} custom-call(f32[256,128]{1,0:T(8,128)} %bitcast.26, f32[256,128]{1,0:T(8,128)} %bitcast.27, f32[256,128]{1,0:T(8,128)} %bitcast.28, f32[128,128]{1,0:T(8,128)} %bitcast.29), custom_call_target="tpu_custom_call" | custom-call | flops 4000000 | bytes 600000 | tf_op jit(solution)/shard_map/line_step/pallas_call | solution.py:580
  24.3 0.7 %copy.6 = f32[2,16,1024]{2,1,0:T(8,128)} copy(f32[2,16,1024]{2,1,0:T(8,128)S(1)} %bitcast.25) | data formatting | bytes 262144

commit v6 on v5

--- a/solution.py
+++ b/solution.py
@@ -11,6 +11,7 @@
 ROWS, SUBS, LANES = 16, 8, 128
 GROUP, OWNERS, PARTS = 16, 8, 64
 FIRST, LAST = 0, 49
+FRONT = (1, 0, 16, 17, 32, 33, 48, 49)
 LOADS, USED, SLOT = 4, 14, 16
 FLAT = 2 * ROWS * SUBS
 
@@ -408,28 +409,33 @@
         @pl.when(solve == column)
         def _():
             wait_for(edge_own, PARTS - 1, own_rsem)
-            wait_for(edge_far, PARTS, far_rsem)
-            sides = []
-            for plane in (0, 1):
-                warm, cond = plane * ROWS, (2 + plane) * ROWS
-                total = along(edge_own, cond) + along(edge_far, cond, inside)
-                step = along(edge_far, warm, inside) - along(edge_own, warm)
-                sides.append(0.5 * total * step)
-                flux_send[pl.ds(plane, SUBS, stride=2), :] = sides[plane]
             first1, first2, second = (along(edge_own, f * ROWS) for f in (4, 5, 6))
             element, way = merge_leaf(
                 second, spin(second, -1), first1, first2, spin(first1, -1), spin(first2, -1)
             )
-            loads, _ = merge_leaf_loads(way, sides, [spin(v, -1) for v in sides])
-            fields = loads + element
+            ways = [way]
             for shift in (2, 4, 8):
-                fields, _, _ = climb(fields, tuple(spin(v, -shift) for v in fields))
+                element, way = merge(element, tuple(spin(v, -shift) for v in element))
+                ways.append(way)
+            own = [along(edge_own, f * ROWS) for f in range(4)]
+            wait_for(edge_far, PARTS, far_rsem)
+            far = [along(edge_far, f * ROWS, inside) for f in range(4)]
+            sides = []
+            for plane in (0, 1):
+                total = own[2 + plane] + far[2 + plane]
+                sides.append(0.5 * total * (far[plane] - own[plane]))
+                flux_send[pl.ds(plane, SUBS, stride=2), :] = sides[plane]
+            fields, _ = merge_leaf_loads(ways[0], sides, [spin(v, -1) for v in sides])
+            for shift, way in zip((2, 4, 8), ways[1:]):
+                fields, _ = merge_loads(way, fields, [spin(v, -shift) for v in fields])
             for a in range(SUBS):
                 for j in range(LOADS):
                     at_rows = pl.ds(a * SUBS * LOADS + j, SUBS, stride=LOADS)
                     moved = spin(fields[j], at - a * ROWS)
                     extra[at_rows, :] = jnp.where(lane == at, moved, 0.0)
-            to_all(0, 16, flux_to(i))
+            for part in FRONT:
+                if part != column:
+                    flux_to(i)(part)
             flux_recv[pl.ds(i * 2, 2), :] = flux_send[pl.ds((column % SUBS) * 2, 2), :]
 
     @pl.when(owner)
@@ -507,7 +513,7 @@
 
         @pl.when(solve == column)
         def _():
-            to_all(16, PARTS, flux_to(i))
+            to_all(OWNERS, PARTS, flux_to(i))
 
     @pl.when(outer)
     def _():

time: 25.1 us -> 25.1 us (level)
  no operation moved by 1% of the time
where the time goes in v6:
time: 25.1 us; the launch traced here: 25 us
  Pallas kernels  24.3 us (97%)
  local copies, waits for them, and re-layouts  0.66 us (3%)
    pallas_call x1, Pallas kernels, per_device(): pl.pallas_call(kernel, out_shape=jax.ShapeDtypeStruct((FLAT, LANES), jnp....  24.3 us
    unnamed x1, local copies, waits for them, and re-layouts  0.66 us

profile of v6, /device:TPU:1, one launch (start us, length us, event | category | flops | bytes accessed | tf_op | source)
XLA Modules:
  0.0 25.0 jit_solution(5820222065968489594)
XLA Ops:
  0.0 24.3 %line_step.1 = f32[256,128]{1,0:T(8,128)S(1)} custom-call(f32[256,128]{1,0:T(8,128)} %bitcast.26, f32[256,128]{1,0:T(8,128)} %bitcast.27, f32[256,128]{1,0:T(8,128)} %bitcast.28, f32[128,128]{1,0:T(8,128)} %bitcast.29), custom_call_target="tpu_custom_call" | custom-call | flops 4000000 | bytes 600000 | tf_op jit(solution)/shard_map/line_step/pallas_call | solution.py:586
  24.3 0.7 %copy.6 = f32[2,16,1024]{2,1,0:T(8,128)} copy(f32[2,16,1024]{2,1,0:T(8,128)S(1)} %bitcast.25) | data formatting | bytes 262144

commit v7 on v5

--- a/solution.py
+++ b/solution.py
@@ -145,7 +145,7 @@
     loads_in = [
         pltpu.make_async_copy(src, dst, in_sem.at[i])
         for i, (src, dst) in enumerate(
-            ((temp_hbm, temp), (diff_hbm, diff), (face_hbm, face), (sheet_hbm, sheet))
+            ((face_hbm, face), (sheet_hbm, sheet), (temp_hbm, temp), (diff_hbm, diff))
         )
     ]
     for copy in loads_in:
@@ -207,60 +207,12 @@
         start = index * rows if isinstance(index, int) else pl.multiple_of(index * rows, rows)
         return ref.at[pl.ds(start, used)]
 
-    for copy in loads_in:
-        copy.wait()
-    tracks = [(ref, j) for ref in (temp, diff, face) for j in range(4)]
-    tracks += [(sheet, 0), (sheet, 1)]
-    for i, (column, shift) in enumerate(((0, 0), (SUBS - 1, 1))):
-        packed = jnp.zeros((SUBS, LANES), jnp.float32)
-        for j, (ref, block) in enumerate(tracks):
-            at = j * SUBS
-            packed = jnp.where(lane == at, spin(tile(ref, block, column), at + shift), packed)
-        for step in (1, 2, 4):
-            packed = packed + spin(pltpu.roll(packed, SUBS - step, 0), step)
-        edge_send[pl.ds(i, 1), :] = packed[0:1, :]
-    flux_recv[pl.ds(4, 4), :] = zero[0:4, :]
-
-    @pl.when(owner)
-    def _():
-        pl.semaphore_wait(barrier, 2 + OWNERS - 1)
-
-    @pl.when(jnp.logical_not(owner))
-    def _():
-        pl.semaphore_wait(barrier, 2 + OWNERS)
-
-    for i, (mine, theirs, side) in enumerate(
-        ((FIRST, LAST, left), (LAST, FIRST, right))
-    ):
-        edge = edge_send.at[pl.ds(i, 1)]
-        pltpu.make_async_remote_copy(
-            src_ref=edge,
-            dst_ref=slot(edge_far, solve, 1, 1),
-            send_sem=edge_ssem,
-            recv_sem=far_rsem,
-            device_id={"solve": theirs, "cross": side},
-            device_id_type=MESH,
-        ).start()
-
-        @pl.when(solve != mine)
-        def _():
-            pltpu.make_async_remote_copy(
-                src_ref=edge,
-                dst_ref=slot(edge_own, solve, 1, 1),
-                send_sem=edge_ssem,
-                recv_sem=own_rsem,
-                device_id={"solve": mine},
-                device_id_type=MESH,
-            ).start()
-
-        @pl.when(solve == mine)
-        def _():
-            edge_own[pl.ds(mine, 1), :] = edge_send[pl.ds(i, 1), :]
-
     def row(ref, plane, i):
         start = (plane * 2 + i // SUBS) * SUBS * SUBS + i % SUBS
         return ref[pl.ds(start, SUBS, stride=SUBS), :]
 
+    loads_in[0].wait()
+    loads_in[1].wait()
     backs = []
     level = []
     back = []
@@ -302,7 +254,57 @@
 
     for j, value in enumerate(element):
         part_send[pl.ds(LOADS + j, SUBS, stride=SLOT), :] = value
+    @pl.when(owner)
+    def _():
+        pl.semaphore_wait(barrier, 2 + OWNERS - 1)
+
+    @pl.when(jnp.logical_not(owner))
+    def _():
+        pl.semaphore_wait(barrier, 2 + OWNERS)
+
     send_parts(part_send, SLOT, LOADS, USED - LOADS)
+
+    loads_in[2].wait()
+    loads_in[3].wait()
+    tracks = [(ref, j) for ref in (temp, diff, face) for j in range(4)]
+    tracks += [(sheet, 0), (sheet, 1)]
+    for i, (column, shift) in enumerate(((0, 0), (SUBS - 1, 1))):
+        packed = jnp.zeros((SUBS, LANES), jnp.float32)
+        for j, (ref, block) in enumerate(tracks):
+            at = j * SUBS
+            packed = jnp.where(lane == at, spin(tile(ref, block, column), at + shift), packed)
+        for step in (1, 2, 4):
+            packed = packed + spin(pltpu.roll(packed, SUBS - step, 0), step)
+        edge_send[pl.ds(i, 1), :] = packed[0:1, :]
+    flux_recv[pl.ds(4, 4), :] = zero[0:4, :]
+
+    for i, (mine, theirs, side) in enumerate(
+        ((FIRST, LAST, left), (LAST, FIRST, right))
+    ):
+        edge = edge_send.at[pl.ds(i, 1)]
+        pltpu.make_async_remote_copy(
+            src_ref=edge,
+            dst_ref=slot(edge_far, solve, 1, 1),
+            send_sem=edge_ssem,
+            recv_sem=far_rsem,
+            device_id={"solve": theirs, "cross": side},
+            device_id_type=MESH,
+        ).start()
+
+        @pl.when(solve != mine)
+        def _():
+            pltpu.make_async_remote_copy(
+                src_ref=edge,
+                dst_ref=slot(edge_own, solve, 1, 1),
+                send_sem=edge_ssem,
+                recv_sem=own_rsem,
+                device_id={"solve": mine},
+                device_id_type=MESH,
+            ).start()
+
+        @pl.when(solve == mine)
+        def _():
+            edge_own[pl.ds(mine, 1), :] = edge_send[pl.ds(i, 1), :]
 
     for block in range(4):
         heat = [tile(temp, block, t) for t in range(SUBS)]

time: 25.1 us -> 25 us (level)
  no operation moved by 1% of the time
where the time goes in v7:
time: 25 us; the launch traced here: 24.9 us
  Pallas kernels  24.2 us (97%)
  local copies, waits for them, and re-layouts  0.66 us (3%)
    pallas_call x1, Pallas kernels, per_device(): pl.pallas_call(kernel, out_shape=jax.ShapeDtypeStruct((FLAT, LANES), jnp....  24.2 us
    unnamed x1, local copies, waits for them, and re-layouts  0.66 us

profile of v7, /device:TPU:1, one launch (start us, length us, event | category | flops | bytes accessed | tf_op | source)
XLA Modules:
  0.0 24.9 jit_solution(9873914368569428681)
XLA Ops:
  0.0 24.2 %line_step.1 = f32[256,128]{1,0:T(8,128)S(1)} custom-call(f32[256,128]{1,0:T(8,128)} %bitcast.26, f32[256,128]{1,0:T(8,128)} %bitcast.27, f32[256,128]{1,0:T(8,128)} %bitcast.28, f32[128,128]{1,0:T(8,128)} %bitcast.29), custom_call_target="tpu_custom_call" | custom-call | flops 4000000 | bytes 600000 | tf_op jit(solution)/shard_map/line_step/pallas_call | solution.py:582
  24.3 0.7 %copy.6 = f32[2,16,1024]{2,1,0:T(8,128)} copy(f32[2,16,1024]{2,1,0:T(8,128)S(1)} %bitcast.25) | data formatting | bytes 262144

commit v8 on v7

--- a/solution.py
+++ b/solution.py
@@ -11,6 +11,7 @@
 ROWS, SUBS, LANES = 16, 8, 128
 GROUP, OWNERS, PARTS = 16, 8, 64
 FIRST, LAST = 0, 49
+FRONT = (1, 0, 16, 17, 32, 33, 48, 49)
 LOADS, USED, SLOT = 4, 14, 16
 FLAT = 2 * ROWS * SUBS
 
@@ -410,28 +411,33 @@
         @pl.when(solve == column)
         def _():
             wait_for(edge_own, PARTS - 1, own_rsem)
-            wait_for(edge_far, PARTS, far_rsem)
-            sides = []
-            for plane in (0, 1):
-                warm, cond = plane * ROWS, (2 + plane) * ROWS
-                total = along(edge_own, cond) + along(edge_far, cond, inside)
-                step = along(edge_far, warm, inside) - along(edge_own, warm)
-                sides.append(0.5 * total * step)
-                flux_send[pl.ds(plane, SUBS, stride=2), :] = sides[plane]
             first1, first2, second = (along(edge_own, f * ROWS) for f in (4, 5, 6))
             element, way = merge_leaf(
                 second, spin(second, -1), first1, first2, spin(first1, -1), spin(first2, -1)
             )
-            loads, _ = merge_leaf_loads(way, sides, [spin(v, -1) for v in sides])
-            fields = loads + element
+            ways = [way]
             for shift in (2, 4, 8):
-                fields, _, _ = climb(fields, tuple(spin(v, -shift) for v in fields))
+                element, way = merge(element, tuple(spin(v, -shift) for v in element))
+                ways.append(way)
+            own = [along(edge_own, f * ROWS) for f in range(4)]
+            wait_for(edge_far, PARTS, far_rsem)
+            far = [along(edge_far, f * ROWS, inside) for f in range(4)]
+            sides = []
+            for plane in (0, 1):
+                total = own[2 + plane] + far[2 + plane]
+                sides.append(0.5 * total * (far[plane] - own[plane]))
+                flux_send[pl.ds(plane, SUBS, stride=2), :] = sides[plane]
+            fields, _ = merge_leaf_loads(ways[0], sides, [spin(v, -1) for v in sides])
+            for shift, way in zip((2, 4, 8), ways[1:]):
+                fields, _ = merge_loads(way, fields, [spin(v, -shift) for v in fields])
             for a in range(SUBS):
                 for j in range(LOADS):
                     at_rows = pl.ds(a * SUBS * LOADS + j, SUBS, stride=LOADS)
                     moved = spin(fields[j], at - a * ROWS)
                     extra[at_rows, :] = jnp.where(lane == at, moved, 0.0)
-            to_all(0, 16, flux_to(i))
+            for part in FRONT:
+                if part != column:
+                    flux_to(i)(part)
             flux_recv[pl.ds(i * 2, 2), :] = flux_send[pl.ds((column % SUBS) * 2, 2), :]
 
     @pl.when(owner)
@@ -509,7 +515,7 @@
 
         @pl.when(solve == column)
         def _():
-            to_all(16, PARTS, flux_to(i))
+            to_all(OWNERS, PARTS, flux_to(i))
 
     @pl.when(outer)
     def _():

time: 25 us -> 25 us (level)
  no operation moved by 1% of the time
where the time goes in v8:
time: 25 us; the launch traced here: 24.9 us
  Pallas kernels  24.2 us (97%)
  local copies, waits for them, and re-layouts  0.66 us (3%)
    pallas_call x1, Pallas kernels, per_device(): pl.pallas_call(kernel, out_shape=jax.ShapeDtypeStruct((FLAT, LANES), jnp....  24.2 us
    unnamed x1, local copies, waits for them, and re-layouts  0.66 us

profile of v8, /device:TPU:1, one launch (start us, length us, event | category | flops | bytes accessed | tf_op | source)
XLA Modules:
  0.0 24.9 jit_solution(11662453473978236057)
XLA Ops:
  0.0 24.2 %line_step.1 = f32[256,128]{1,0:T(8,128)S(1)} custom-call(f32[256,128]{1,0:T(8,128)} %bitcast.26, f32[256,128]{1,0:T(8,128)} %bitcast.27, f32[256,128]{1,0:T(8,128)} %bitcast.28, f32[128,128]{1,0:T(8,128)} %bitcast.29), custom_call_target="tpu_custom_call" | custom-call | flops 4000000 | bytes 600000 | tf_op jit(solution)/shard_map/line_step/pallas_call | solution.py:588
  24.3 0.7 %copy.6 = f32[2,16,1024]{2,1,0:T(8,128)} copy(f32[2,16,1024]{2,1,0:T(8,128)S(1)} %bitcast.25) | data formatting | bytes 262144
